TPU v7x, 32 devices: a whole 2x2x4 slice. The times are simulated.
32 devices in a mesh: section: 4 (over x, core), dp: 8 (over z, y).
Axes of the slice: x: 2, y: 2, z: 4, core: 2. Of those that a mesh axis runs over, the one named last changes fastest.
Arguments:
- section_input: bfloat16 [3, 16, 6656], P(None, 'dp'), may hold values from -6 to 6
- out_cotangent: bfloat16 [3, 16, 6656], P(None, 'dp'), may hold values from -18 to 18
- up_weight: bfloat16 [4, 6656, 8960], P('section', None, 'dp'), may hold values from -6 to 6
- down_weight: bfloat16 [4, 6656, 8960], P('section', None, 'dp'), may hold values from -6 to 6
- norm_gain: float32 [4, 6656], P('section'), may hold values from 0.25 to 1.75
Outputs:
- grad_up: float32 [4, 6656, 8960], P('section', None, 'dp')
- grad_down: float32 [4, 6656, 8960], P('section', None, 'dp')
- grad_gain: float32 [4, 6656], P('section')
All inputs are finite; a program needn't handle non-finite values.
Results may differ from a plain program's by a relative error of at most 0.03.
Values may be sent and summed in bfloat16 or wider, within the bound.
No kernel may reach another device: no remote copies, remote signals or barrier semaphores. Data moves between devices by JAX's collectives and lax.ppermute only.
A program may use at most 384 MiB of HBM per device.

v0:
```python
import math

import jax
import jax.numpy as jnp
from jax import lax
from jax.sharding import PartitionSpec as P

D = 6656
HIDDEN_SIZE = 8960


EPSILON = 1e-05
GELU_SCALE = 0.7978845608028654
GELU_CUBIC = 0.044715


def shifted(value, axis, steps):
    count = lax.axis_size(axis)
    leading, last = (max(0, -steps), min(count, count - steps))
    return lax.ppermute(value, axis, [(source, source + steps) for source in range(leading, last)])


def gelu_value(preact):
    inner = GELU_SCALE * (preact + GELU_CUBIC * preact * preact * preact)
    return 0.5 * preact * (1.0 + jnp.tanh(inner))


def gelu_slope(preact):
    inner = GELU_SCALE * (preact + GELU_CUBIC * preact * preact * preact)
    tangent = jnp.tanh(inner)
    return 0.5 * (1.0 + tangent) + 0.5 * preact * (1.0 - tangent * tangent) * GELU_SCALE * (
        1.0 + 3.0 * GELU_CUBIC * preact * preact
    )


def normalize(tok_rows):
    values = tok_rows.astype(jnp.float32)
    norm_scale = lax.rsqrt(jnp.mean(values * values, axis=-1, keepdims=True) + EPSILON)
    return (values, norm_scale, values * norm_scale)


def store(buffer, micro_slot, is_valid, fresh):
    current = lax.dynamic_index_in_dim(buffer, micro_slot, 0, keepdims=False)
    chosen = jnp.where(is_valid, fresh, current)
    return lax.dynamic_update_index_in_dim(buffer, chosen, micro_slot, 0)


def fetch(buffer, micro_slot):
    return lax.dynamic_index_in_dim(buffer, micro_slot, 0, keepdims=False)


def outer_rows(left, right):
    return lax.dot_general(
        left, right, (((0,), (0,)), ((), ())), preferred_element_type=jnp.float32
    )


def across_hidden(left, right):
    return lax.dot_general(
        left, right, (((1,), (1,)), ((), ())), preferred_element_type=jnp.float32
    )


def body(section_input, out_cotangent, up_weight, down_weight, norm_gain):
    section_count = lax.axis_size("section")
    section_pos = lax.axis_index("section")
    micro_count = section_input.shape[0]
    tick_count = micro_count + section_count - 1
    weight_up = up_weight[0]
    weight_down = down_weight[0]
    gain_row = norm_gain[0]
    model_width = weight_up.shape[0]
    local_hidden = weight_up.shape[1]
    full_rows = section_input.shape[1] * lax.axis_size("dp")
    inv_width = 1.0 / math.sqrt(D)
    inv_hidden = 1.0 / math.sqrt(HIDDEN_SIZE)
    entry_all, final_all = (
        lax.all_gather(section_input, "dp", axis=1, tiled=True),
        lax.all_gather(out_cotangent, "dp", axis=1, tiled=True),
    )
    stash_rows = jnp.zeros_like(entry_all)
    stash_scaled = jnp.zeros((micro_count, full_rows, model_width), jnp.bfloat16)
    stash_preact = jnp.zeros((micro_count, full_rows, local_hidden), jnp.float32)
    stash_hidden = jnp.zeros((micro_count, full_rows, local_hidden), jnp.bfloat16)
    incoming = jnp.zeros_like(entry_all[0])
    for clock_tick in range(tick_count):
        entry_rows = entry_all[min(clock_tick, micro_count - 1)]
        tok_rows = jnp.where(section_pos == 0, entry_rows, incoming)
        micro_slot = clock_tick - section_pos
        is_valid = (micro_slot >= 0) & (micro_slot < micro_count)
        micro_slot = jnp.clip(micro_slot, 0, micro_count - 1)
        values, norm_scale, normed = normalize(tok_rows)
        scaled = (normed * gain_row).astype(jnp.bfloat16)
        scaled_all = scaled
        preact = jnp.dot(scaled_all, weight_up, preferred_element_type=jnp.float32) * inv_width
        hidden = gelu_value(preact).astype(jnp.bfloat16)
        partial_value = across_hidden(hidden, weight_down) * inv_hidden
        branch = lax.psum(partial_value.astype(jnp.bfloat16), "dp").astype(jnp.float32)
        result = (values + branch).astype(jnp.bfloat16)
        stash_rows = store(stash_rows, micro_slot, is_valid, tok_rows)
        stash_scaled = store(stash_scaled, micro_slot, is_valid, scaled_all)
        stash_preact = store(stash_preact, micro_slot, is_valid, preact)
        stash_hidden = store(stash_hidden, micro_slot, is_valid, hidden)
        incoming = shifted(result, "section", 1)
    acc_up = jnp.zeros((model_width, local_hidden), jnp.float32)
    acc_down = jnp.zeros((model_width, local_hidden), jnp.float32)
    acc_gain = jnp.zeros((model_width,), jnp.float32)
    incoming = jnp.zeros_like(final_all[0])
    for clock_tick in range(tick_count):
        final_grad = final_all[min(clock_tick, micro_count - 1)]
        grad_rows = jnp.where(section_pos == section_count - 1, final_grad, incoming)
        micro_slot = clock_tick - (section_count - 1 - section_pos)
        is_valid = (micro_slot >= 0) & (micro_slot < micro_count)
        micro_slot = jnp.clip(micro_slot, 0, micro_count - 1)
        block_in = fetch(stash_rows, micro_slot)
        scaled_all = fetch(stash_scaled, micro_slot)
        preact = fetch(stash_preact, micro_slot)
        hidden = fetch(stash_hidden, micro_slot)
        hidden_grad = (
            jnp.dot(grad_rows, weight_down, preferred_element_type=jnp.float32) * inv_hidden
        )
        preact_grad = (hidden_grad * gelu_slope(preact)).astype(jnp.bfloat16)
        scaled_part = across_hidden(preact_grad, weight_up) * inv_width
        scaled_grad = lax.psum(scaled_part.astype(jnp.bfloat16), "dp").astype(jnp.float32)
        values, norm_scale, normed = normalize(block_in)
        gain_term = jnp.sum(scaled_grad * normed, axis=0)
        normed_grad = scaled_grad * gain_row
        input_grad = grad_rows.astype(jnp.float32) + norm_scale * (
            normed_grad - normed * jnp.mean(normed_grad * normed, axis=-1, keepdims=True)
        )
        acc_down = jnp.where(
            is_valid, acc_down + outer_rows(grad_rows, hidden) * inv_hidden, acc_down
        )
        acc_up = jnp.where(
            is_valid, acc_up + outer_rows(scaled_all, preact_grad) * inv_width, acc_up
        )
        acc_gain = jnp.where(is_valid, acc_gain + gain_term, acc_gain)
        incoming = shifted(input_grad.astype(jnp.bfloat16), "section", -1)
    return (acc_up[None], acc_down[None], acc_gain[None])


def solution(mesh):
    placed = (
        P(None, "dp", None),
        P(None, "dp", None),
        P("section", None, "dp"),
        P("section", None, "dp"),
        P("section", None),
    )
    return jax.shard_map(
        body,
        mesh=mesh,
        in_specs=placed,
        out_specs=(P("section", None, "dp"), P("section", None, "dp"), P("section", None)),
        check_vma=False,
    )
```

profile of v0, /device:TPU:0, one launch (start us, length us, event | category | flops | bytes accessed | tf_op | source)
XLA Modules:
  0.0 1158.8 jit_solution(11477036288501990131)
XLA Ops:
  8.2 34.0 %all_gather.6 = bf16[3,16,6656]{2,0,1:T(4,128)(2,1)S(1)} all-gather(bf16[3,2,6656]{2,0,1:T(4,128)(2,1)S(1)} %copy.8), channel_id=1, replica_groups=mesh['section'=4,'dp'=8] {'dp'}, dimensions={1}, use_global_device_ids=true | all-gather | bytes 718848 | tf_op jit(solution)/shard_map/all_gather | solution.py:78
  45.1 9.2 bitcast_dynamic-update-slice_fusion.15
  62.5 32.5 %all_gather.7 = bf16[3,16,6656]{2,0,1:T(4,128)(2,1)S(1)} all-gather(bf16[3,2,6656]{2,0,1:T(4,128)(2,1)S(1)} %copy.12), channel_id=1, replica_groups=mesh['section'=4,'dp'=8] {'dp'}, dimensions={1}, use_global_device_ids=true | all-gather | bytes 718848 | tf_op jit(solution)/shard_map/all_gather | solution.py:79
  97.0 39.0 %all-reduce.12.cloned.1.call-done = bf16[16,6656]{1,0:T(8,128)(2,1)} async-done(((bf16[16,6656]{1,0:T(8,128)(2,1)}), bf16[16,6656]{1,0:T(8,128)(2,1)}) %all-reduce.12.cloned.1.call-update) | async-done | bytes 213008 | tf_op jit(solution)/shard_map/psum | solution.py:98
  159.5 73.2 %all-reduce.14.cloned.1.call-done = bf16[16,6656]{1,0:T(8,128)(2,1)} async-done(((bf16[16,6656]{1,0:T(8,128)(2,1)}), bf16[16,6656]{1,0:T(8,128)(2,1)}) %all-reduce.14.cloned.1.call-update) | async-done | bytes 213008 | tf_op jit(solution)/shard_map/psum | solution.py:98
  257.1 73.1 %all-reduce.16.cloned.1.call-done = bf16[16,6656]{1,0:T(8,128)(2,1)} async-done(((bf16[16,6656]{1,0:T(8,128)(2,1)}), bf16[16,6656]{1,0:T(8,128)(2,1)}) %all-reduce.16.cloned.1.call-update) | async-done | bytes 213008 | tf_op jit(solution)/shard_map/psum | solution.py:98
  335.0 9.2 bitcast_dynamic-update-slice_fusion.12
  353.7 73.1 %all-reduce.18.cloned.1.call-done = bf16[16,6656]{1,0:T(8,128)(2,1)} async-done(((bf16[16,6656]{1,0:T(8,128)(2,1)}), bf16[16,6656]{1,0:T(8,128)(2,1)}) %all-reduce.18.cloned.1.call-update) | async-done | bytes 213008 | tf_op jit(solution)/shard_map/psum | solution.py:98
  450.3 73.2 %all-reduce.20.cloned.1.call-done = bf16[16,6656]{1,0:T(8,128)(2,1)} async-done(((bf16[16,6656]{1,0:T(8,128)(2,1)}), bf16[16,6656]{1,0:T(8,128)(2,1)}) %all-reduce.20.cloned.1.call-update) | async-done | bytes 213008 | tf_op jit(solution)/shard_map/psum | solution.py:98
  537.6 9.2 fusion.167
  555.0 12.6 %fusion.1 = f32[6656,1120]{0,1:T(8,128)} fusion(pred[]{:T(512)S(6)} %and.42, bf16[3,16,1120]{2,1,0:T(8,128)(2,1)S(1)} %bitcast_dynamic-update-slice_fusion.16, s32[]{:T(128)S(6)} %min.43, bf16[1,16,6656]{2,0,1:T(2,128)(2,1)S(1)} %get-tuple-element.35, pred[]{:T(512)S(6)} %eq.5), kind=kOutput, calls=%fused_computation.23 | convolution fusion | flops 253566976 | bytes 30281734 | tf_op jit(solution)/shard_map/dot_general | solution.py:53
  567.6 12.6 %fusion = f32[6656,1120]{0,1:T(8,128)} fusion(bf16[16,1120]{1,0:T(8,128)(2,1)S(1)} %fusion.167, pred[]{:T(512)S(6)} %and.42, bf16[3,16,6656]{2,1,0:T(8,128)(2,1)S(1)} %bitcast_dynamic-update-slice_fusion.5, s32[]{:T(128)S(6)} %min.43), kind=kOutput, calls=%fused_computation.22 | convolution fusion | flops 253460480 | bytes 30068740 | tf_op jit(solution)/shard_map/dot_general | solution.py:53
  580.2 49.2 %all-reduce.22.cloned.1.call-done = bf16[16,6656]{1,0:T(8,128)(2,1)} async-done(((bf16[16,6656]{1,0:T(8,128)(2,1)}), bf16[16,6656]{1,0:T(8,128)(2,1)}) %all-reduce.22.cloned.1.call-update) | async-done | bytes 213008 | tf_op jit(solution)/shard_map/psum | solution.py:124
  636.6 9.2 fusion.164
  653.9 19.7 %add_select_fusion.4 = f32[6656,1120]{0,1:T(8,128)} fusion(f32[6656,1120]{0,1:T(8,128)} %fusion.1, bf16[16,6656]{1,0:T(8,128)(2,1)S(1)} %fusion.248, pred[]{:T(512)S(6)} %and.41, bf16[3,16,1120]{2,1,0:T(8,128)(2,1)S(1)} %bitcast_dynamic-update-slice_fusion.16, s32[]{:T(128)S(6)} %min.44), kind=kOutput, calls=%fused_computation.4 | convolution fusion | flops 260915200 | bytes 59887620 | tf_op jit(solution)/shard_map/dot_general | solution.py:53
  673.6 52.4 %all-reduce.24.cloned.1.call-done = bf16[16,6656]{1,0:T(8,128)(2,1)} async-done(((bf16[16,6656]{1,0:T(8,128)(2,1)}), bf16[16,6656]{1,0:T(8,128)(2,1)}) %all-reduce.24.cloned.1.call-update) | async-done | bytes 213008 | tf_op jit(solution)/shard_map/psum | solution.py:124
  730.2 19.8 %add_select_fusion.9 = f32[6656,1120]{0,1:T(8,128)} fusion(f32[6656,1120]{0,1:T(8,128)} %fusion, bf16[16,1120]{1,0:T(8,128)(2,1)S(1)} %fusion.164, pred[]{:T(512)S(6)} %and.41, bf16[3,16,6656]{2,1,0:T(8,128)(2,1)S(1)} %bitcast_dynamic-update-slice_fusion.5, s32[]{:T(128)S(6)} %min.44), kind=kOutput, calls=%fused_computation.9 | convolution fusion | flops 260915200 | bytes 59887620 | tf_op jit(solution)/shard_map/dot_general | solution.py:53
  750.1 9.2 fusion.161
  767.5 20.1 %add_select_fusion.8 = f32[6656,1120]{0,1:T(8,128)} fusion(f32[6656,1120]{0,1:T(8,128)} %add_select_fusion.9, bf16[16,1120]{1,0:T(8,128)(2,1)S(1)} %fusion.161, pred[]{:T(512)S(6)} %and.40, bf16[3,16,6656]{2,1,0:T(8,128)(2,1)S(1)} %bitcast_dynamic-update-slice_fusion.5, s32[]{:T(128)S(6)} %min.45), kind=kOutput, calls=%fused_computation.8 | convolution fusion | flops 260915200 | bytes 59887620 | tf_op jit(solution)/shard_map/dot_general | solution.py:53
  787.6 50.2 %all-reduce.26.cloned.1.call-done = bf16[16,6656]{1,0:T(8,128)(2,1)} async-done(((bf16[16,6656]{1,0:T(8,128)(2,1)}), bf16[16,6656]{1,0:T(8,128)(2,1)}) %all-reduce.26.cloned.1.call-update) | async-done | bytes 213008 | tf_op jit(solution)/shard_map/psum | solution.py:124
  842.0 11.9 %convolution_multiply_fusion.3 = f32[6656,1120]{0,1:T(8,128)} fusion(bf16[16,6656]{1,0:T(8,128)(2,1)S(1)} %get-tuple-element.18, bf16[3,16,1120]{2,1,0:T(8,128)(2,1)S(1)} %bitcast_dynamic-update-slice_fusion.16, s32[]{:T(128)S(6)} %min.45), kind=kOutput, calls=%fused_computation.13 | convolution fusion | flops 246005760 | bytes 30068740 | tf_op jit(solution)/shard_map/dot_general | solution.py:53
  854.0 9.2 fusion.158
  871.2 20.1 %add_select_fusion.7 = f32[6656,1120]{0,1:T(8,128)} fusion(f32[6656,1120]{0,1:T(8,128)} %add_select_fusion.8, bf16[16,1120]{1,0:T(8,128)(2,1)S(1)} %fusion.158, pred[]{:T(512)S(6)} %and.39, bf16[3,16,6656]{2,1,0:T(8,128)(2,1)S(1)} %bitcast_dynamic-update-slice_fusion.5, s32[]{:T(128)S(6)} %min.46), kind=kOutput, calls=%fused_computation.7 | convolution fusion | flops 260915200 | bytes 59887620 | tf_op jit(solution)/shard_map/dot_general | solution.py:53
  891.3 50.4 %all-reduce.28.cloned.1.call-done = bf16[16,6656]{1,0:T(8,128)(2,1)} async-done(((bf16[16,6656]{1,0:T(8,128)(2,1)}), bf16[16,6656]{1,0:T(8,128)(2,1)}) %all-reduce.28.cloned.1.call-update) | async-done | bytes 213008 | tf_op jit(solution)/shard_map/psum | solution.py:124
  945.7 12.1 %convolution_multiply_fusion.2 = f32[6656,1120]{0,1:T(8,128)} fusion(bf16[16,6656]{1,0:T(8,128)(2,1)S(1)} %broadcast_select_fusion.2, bf16[3,16,1120]{2,1,0:T(8,128)(2,1)S(1)} %bitcast_dynamic-update-slice_fusion.16, s32[]{:T(128)S(6)} %min.46), kind=kOutput, calls=%fused_computation.12 | convolution fusion | flops 246005760 | bytes 30068740 | tf_op jit(solution)/shard_map/dot_general | solution.py:53
  957.8 9.2 fusion.155
  975.1 20.1 %add_select_fusion.6 = f32[6656,1120]{0,1:T(8,128)} fusion(f32[6656,1120]{0,1:T(8,128)} %add_select_fusion.7, bf16[16,1120]{1,0:T(8,128)(2,1)S(1)} %fusion.155, pred[]{:T(512)S(6)} %and.38, bf16[3,16,6656]{2,1,0:T(8,128)(2,1)S(1)} %bitcast_dynamic-update-slice_fusion.5, s32[]{:T(128)S(6)} %min.47), kind=kOutput, calls=%fused_computation.6 | convolution fusion | flops 260915200 | bytes 59887620 | tf_op jit(solution)/shard_map/dot_general | solution.py:53
  995.2 50.4 %all-reduce.30.cloned.1.call-done = bf16[16,6656]{1,0:T(8,128)(2,1)} async-done(((bf16[16,6656]{1,0:T(8,128)(2,1)}), bf16[16,6656]{1,0:T(8,128)(2,1)}) %all-reduce.30.cloned.1.call-update) | async-done | bytes 213008 | tf_op jit(solution)/shard_map/psum | solution.py:124
  1049.6 12.6 %convolution_multiply_fusion.1 = f32[6656,1120]{0,1:T(8,128)} fusion(bf16[16,6656]{1,0:T(8,128)(2,1)S(1)} %broadcast_select_fusion.1, bf16[3,16,1120]{2,1,0:T(8,128)(2,1)S(1)} %bitcast_dynamic-update-slice_fusion.16, s32[]{:T(128)S(6)} %min.47), kind=kOutput, calls=%fused_computation.11 | convolution fusion | flops 246005760 | bytes 30068740 | tf_op jit(solution)/shard_map/dot_general | solution.py:53
  1062.2 9.2 fusion.152
  1079.4 48.5 %fusion.3 = f32[1,6656,1120]{1,2,0:T(8,128)} fusion(f32[6656,1120]{0,1:T(8,128)} %convolution_multiply_fusion.1, f32[6656,1120]{0,1:T(8,128)} %convolution_multiply_fusion.2, f32[6656,1120]{0,1:T(8,128)} %add_select_fusion.4, f32[6656,1120]{0,1:T(8,128)} %convolution_multiply_fusion.3, pred[]{:T(512)S(6)} %and.40, pred[]{:T(512)S(6)} %and.39, ...), kind=kOutput, calls=%fused_computation.25 | convolution fusion | flops 305750016 | bytes 149557264 | tf_op jit(solution)/shard_map/dot_general | solution.py:53
  1128.0 20.0 %fusion.2 = f32[1,6656,1120]{1,2,0:T(8,128)} fusion(f32[6656,1120]{0,1:T(8,128)} %add_select_fusion.6, bf16[16,1120]{1,0:T(8,128)(2,1)S(1)} %fusion.152, pred[]{:T(512)S(6)} %and.37, bf16[3,16,6656]{2,1,0:T(8,128)(2,1)S(1)} %bitcast_dynamic-update-slice_fusion.5, s32[]{:T(128)S(6)} %min.48), kind=kOutput, calls=%fused_computation.24 | convolution fusion | flops 260915200 | bytes 59887620 | tf_op jit(solution)/shard_map/dot_general | solution.py:53
  (173 shorter events, 189.3 us)
Async XLA Ops:
  7.2 128.8 %all-reduce.12.cloned.1.call-start = ((), (), s32[]{:S(2)}) async-start(), calls=%async_computation | async-start | bytes 425984 | tf_op jit(solution)/shard_map/psum | solution.py:98
  45.1 17.4 %copy-start.8 = (bf16[3,2,6656]{2,1,0:T(2,128)(2,1)S(1)}, bf16[3,2,6656]{2,1,0:T(2,128)(2,1)}, u32[]{:S(2)}) copy-start(bf16[3,2,6656]{2,1,0:T(2,128)(2,1)} %param.6) | copy-start | bytes 239620
  62.3 170.3 %all-reduce.14.cloned.1.call-start = ((), (), s32[]{:S(2)}) async-start(), calls=%async_computation.1 | async-start | bytes 425984 | tf_op jit(solution)/shard_map/psum | solution.py:98
  136.9 2.4 collective-permute-start
  140.8 17.2 %copy-start.2 = (bf16[1,16,1120]{2,1,0:T(8,128)(2,1)S(1)}, bf16[1,16,1120]{2,1,0:T(8,128)(2,1)}, u32[]{:S(2)}) copy-start(bf16[1,16,1120]{2,1,0:T(8,128)(2,1)} %constant_dynamic-slice_fusion.4) | copy-start | bytes 107524
  158.1 172.2 %all-reduce.16.cloned.1.call-start = ((), (), s32[]{:S(2)}) async-start(), calls=%async_computation.2 | async-start | bytes 425984 | tf_op jit(solution)/shard_map/psum | solution.py:98
  233.6 2.4 collective-permute-start.1
  238.4 17.2 %copy-start.1 = (bf16[1,16,1120]{2,1,0:T(8,128)(2,1)S(1)}, bf16[1,16,1120]{2,1,0:T(8,128)(2,1)}, u32[]{:S(2)}) copy-start(bf16[1,16,1120]{2,1,0:T(8,128)(2,1)} %constant_dynamic-slice_fusion.3) | copy-start | bytes 107524
  255.7 171.2 %all-reduce.18.cloned.1.call-start = ((), (), s32[]{:S(2)}) async-start(), calls=%async_computation.3 | async-start | bytes 425984 | tf_op jit(solution)/shard_map/psum | solution.py:98
  331.2 2.4 collective-permute-start.2
  335.0 17.2 %copy-start.3 = (bf16[1,16,1120]{2,1,0:T(8,128)(2,1)S(1)}, bf16[1,16,1120]{2,1,0:T(8,128)(2,1)}, u32[]{:S(2)}) copy-start(bf16[1,16,1120]{2,1,0:T(8,128)(2,1)} %constant_dynamic-slice_fusion.2) | copy-start | bytes 107524
  352.3 171.2 %all-reduce.20.cloned.1.call-start = ((), (), s32[]{:S(2)}) async-start(), calls=%async_computation.4 | async-start | bytes 425984 | tf_op jit(solution)/shard_map/psum | solution.py:98
  427.8 2.4 collective-permute-start.3
  431.6 17.2 %copy-start.4 = (bf16[1,16,1120]{2,1,0:T(8,128)(2,1)S(1)}, bf16[1,16,1120]{2,1,0:T(8,128)(2,1)}, u32[]{:S(2)}) copy-start(bf16[1,16,1120]{2,1,0:T(8,128)(2,1)} %constant_dynamic-slice_fusion.1) | copy-start | bytes 107524
  448.9 180.5 %all-reduce.22.cloned.1.call-start = ((), (), s32[]{:S(2)}) async-start(), calls=%async_computation.5 | async-start | bytes 425984 | tf_op jit(solution)/shard_map/psum | solution.py:124
  524.5 2.4 collective-permute-start.4
  537.6 17.3 %copy-start = (bf16[1,16,1120]{2,1,0:T(8,128)(2,1)S(1)}, bf16[1,16,1120]{2,1,0:T(8,128)(2,1)}, u32[]{:S(2)}) copy-start(bf16[1,16,1120]{2,1,0:T(8,128)(2,1)} %constant_dynamic-slice_fusion) | copy-start | bytes 107524
  554.8 171.2 %all-reduce.24.cloned.1.call-start = ((), (), s32[]{:S(2)}) async-start(), calls=%async_computation.6 | async-start | bytes 425984 | tf_op jit(solution)/shard_map/psum | solution.py:124
  633.2 3.4 collective-permute-start.5
  653.8 184.0 %all-reduce.26.cloned.1.call-start = ((), (), s32[]{:S(2)}) async-start(), calls=%async_computation.7 | async-start | bytes 425984 | tf_op jit(solution)/shard_map/psum | solution.py:124
  728.9 21.1 %collective-permute-start.6 = (bf16[16,6656]{1,0:T(8,128)(2,1)S(1)}, bf16[16,6656]{1,0:T(8,128)(2,1)S(1)}, u32[]{:S(2)}, u32[]{:S(2)}) collective-permute-start(bf16[16,6656]{1,0:T(8,128)(2,1)S(1)} %fusion.203), channel_id=1, source_target_pairs={{8,0},{16,8},{24,16},{9,1},{17,9},{25,17},{10,2},{18,10},{26,18},{... | collective-permute-start | bytes 638984 | tf_op jit(solution)/shard_map/ppermute | solution.py:20
  767.3 174.5 %all-reduce.28.cloned.1.call-start = ((), (), s32[]{:S(2)}) async-start(), calls=%async_computation.8 | async-start | bytes 425984 | tf_op jit(solution)/shard_map/psum | solution.py:124
  840.7 13.2 %collective-permute-start.7 = (bf16[16,6656]{1,0:T(8,128)(2,1)S(1)}, bf16[16,6656]{1,0:T(8,128)(2,1)S(1)}, u32[]{:S(2)}, u32[]{:S(2)}) collective-permute-start(bf16[16,6656]{1,0:T(8,128)(2,1)S(1)} %fusion.200), channel_id=1, source_target_pairs={{8,0},{16,8},{24,16},{9,1},{17,9},{25,17},{10,2},{18,10},{26,18},{... | collective-permute-start | bytes 638984 | tf_op jit(solution)/shard_map/ppermute | solution.py:20
  871.2 174.4 %all-reduce.30.cloned.1.call-start = ((), (), s32[]{:S(2)}) async-start(), calls=%async_computation.9 | async-start | bytes 425984 | tf_op jit(solution)/shard_map/psum | solution.py:124
  944.2 13.6 %collective-permute-start.8 = (bf16[16,6656]{1,0:T(8,128)(2,1)S(1)}, bf16[16,6656]{1,0:T(8,128)(2,1)S(1)}, u32[]{:S(2)}, u32[]{:S(2)}) collective-permute-start(bf16[16,6656]{1,0:T(8,128)(2,1)S(1)} %fusion.197), channel_id=1, source_target_pairs={{8,0},{16,8},{24,16},{9,1},{17,9},{25,17},{10,2},{18,10},{26,18},{... | collective-permute-start | bytes 638984 | tf_op jit(solution)/shard_map/ppermute | solution.py:20
  975.1 70.6 %copy-start.9 = (f32[16]{0:T(128)S(1)}, f32[16]{0:T(128)}, u32[]{:S(2)}) copy-start(f32[16]{0:T(128)} %add_rsqrt_fusion.1) | copy-start | bytes 196
  975.1 174.9 %all-reduce.32.cloned.1.call-start = ((), (), s32[]{:S(2)}) async-start(), calls=%async_computation.10 | async-start | bytes 425984 | tf_op jit(solution)/shard_map/psum | solution.py:124
  1048.0 14.2 %collective-permute-start.9 = (bf16[16,6656]{1,0:T(8,128)(2,1)S(1)}, bf16[16,6656]{1,0:T(8,128)(2,1)S(1)}, u32[]{:S(2)}, u32[]{:S(2)}) collective-permute-start(bf16[16,6656]{1,0:T(8,128)(2,1)S(1)} %fusion.194), channel_id=1, source_target_pairs={{8,0},{16,8},{24,16},{9,1},{17,9},{25,17},{10,2},{18,10},{26,18},{... | collective-permute-start | bytes 638984 | tf_op jit(solution)/shard_map/ppermute | solution.py:20
  1128.0 22.0 %copy-start.10 = (f32[16]{0:T(128)S(1)}, f32[16]{0:T(128)}, u32[]{:S(2)}) copy-start(f32[16]{0:T(128)} %add_rsqrt_fusion) | copy-start | bytes 196
  1128.0 23.2 %copy-start.5 = (f32[6656]{0:T(1024)S(1)}, f32[6656]{0:T(1024)}, u32[]{:S(2)}) copy-start(f32[6656]{0:T(1024)} %broadcast_select_fusion.15) | copy-start | bytes 79876
  1128.0 23.2 %copy-start.6 = (f32[6656]{0:T(1024)S(1)}, f32[6656]{0:T(1024)}, u32[]{:S(2)}) copy-start(f32[6656]{0:T(1024)} %get-tuple-element.5) | copy-start | bytes 79876
  1128.0 23.2 %copy-start.7 = (f32[6656]{0:T(1024)S(1)}, f32[6656]{0:T(1024)}, u32[]{:S(2)}) copy-start(f32[6656]{0:T(1024)} %get-tuple-element.7) | copy-start | bytes 79876
Sparse Core Ops, SparseCore 0:
  62.5 73.4 all-reduce.11
  158.2 74.3 all-reduce.13
  255.8 74.3 all-reduce.15
  352.4 74.3 all-reduce.17
  449.0 74.4 all-reduce.19
  555.0 74.3 all-reduce.21
  653.9 72.0 all-reduce.23
  767.4 70.3 all-reduce.25
  871.3 70.4 all-reduce.27
  975.2 70.3 all-reduce.29
  1079.6 70.3 all-reduce.31
where the time goes:
time: 1170 us; the launch traced here: 1160 us
  waiting for transfers between devices  590 us (50%)
  matrix products  429 us (37%)
  blocking collectives  66.5 us (6%)
  other arithmetic  31.2 us (3%)
  starting transfers between devices  14.9 us (1%)
  between operations  14.9 us (1%)
  local copies, waits for them, and re-layouts  13.1 us (1%)
    psum x5, waiting for transfers between devices, body(): lax.psum(partial_value.astype(jnp.bfloat16), 'dp').astype(jnp.float32)  332 us
    psum x6, waiting for transfers between devices, body(): lax.psum(scaled_part.astype(jnp.bfloat16), 'dp').astype(jnp.float32)  255 us
    dot_general x12, matrix products, outer_rows(): lax.dot_general(left, right, (((0,), (0,)), ((), ())), preferred_element_...  230 us
    dot_general x11, matrix products, across_hidden(): lax.dot_general(left, right, (((1,), (1,)), ((), ())), preferred_element_...  88.3 us
    dot_general x6, matrix products, body(): jnp.dot(grad_rows, weight_down, preferred_element_type=jnp.float32)  55.2 us
    dot_general x6, matrix products, body(): jnp.dot(scaled_all, weight_up, preferred_element_type=jnp.float32)  55.2 us
    all_gather x1, blocking collectives, body(): lax.all_gather(section_input, 'dp', axis=1, tiled=True)  34 us
    all_gather x1, blocking collectives, body(): lax.all_gather(out_cotangent, 'dp', axis=1, tiled=True)  32.5 us
  transfers between devices with their start and end apart: 21, of which 17 were waited for; matrix products, arithmetic and copies ran while one was open for 21% of the time, Pallas kernels for 0%

commit v1 on v0

v1 whole, which is shorter than its diff:
```python
import math

import jax
import jax.numpy as jnp
from jax import lax
from jax.sharding import PartitionSpec as P

D = 6656
HIDDEN_SIZE = 8960


EPSILON = 1e-05
GELU_SCALE = 0.7978845608028654
GELU_CUBIC = 0.044715

AXES = ("section", "dp")


def gelu_value(preact):
    inner = GELU_SCALE * (preact + GELU_CUBIC * preact * preact * preact)
    return 0.5 * preact * (1.0 + jnp.tanh(inner))


def gelu_slope(preact):
    inner = GELU_SCALE * (preact + GELU_CUBIC * preact * preact * preact)
    tangent = jnp.tanh(inner)
    return 0.5 * (1.0 + tangent) + 0.5 * preact * (1.0 - tangent * tangent) * GELU_SCALE * (
        1.0 + 3.0 * GELU_CUBIC * preact * preact
    )


def normalize(tok_rows):
    values = tok_rows.astype(jnp.float32)
    norm_scale = lax.rsqrt(jnp.mean(values * values, axis=-1, keepdims=True) + EPSILON)
    return (values, norm_scale, values * norm_scale)


def outer_rows(left, right):
    return lax.dot_general(
        left, right, (((0,), (0,)), ((), ())), preferred_element_type=jnp.float32
    )


def across_hidden(left, right):
    return lax.dot_general(
        left, right, (((1,), (1,)), ((), ())), preferred_element_type=jnp.float32
    )


def send(value, source, target, step):
    count = lax.axis_size("dp")
    if source == target and step % count == 0:
        return value
    return lax.ppermute(
        value,
        AXES,
        [(source * count + r, target * count + (r + step) % count) for r in range(count)],
    )


def spread(chunk, source, target):
    return jnp.concatenate(
        [send(chunk, source, target, k) for k in range(lax.axis_size("dp"))], axis=0
    )


def collect(parts, section):
    count = lax.axis_size("dp")
    pieces = parts.reshape(count, -1, parts.shape[-1])
    total = pieces[0].astype(jnp.float32)
    for k in range(1, count):
        total = total + send(pieces[k], section, section, -k).astype(jnp.float32)
    return total


def collect_all(parts):
    count = lax.axis_size("dp")
    pieces = parts.reshape(count, -1, parts.shape[-1])
    backward = jnp.concatenate([pieces[:1], pieces[:0:-1]], axis=0)
    doubled = jnp.concatenate([backward, backward], axis=0)
    offset = (count - lax.axis_index("dp")) % count
    placed = lax.dynamic_slice_in_dim(doubled, offset, count, 0)
    arrived = lax.all_to_all(placed, "dp", 0, 0, tiled=True)
    return jnp.sum(arrived.astype(jnp.float32), axis=0)


def sum_over_dp(value):
    count = lax.axis_size("dp")
    if count & (count - 1):
        return lax.psum(value, "dp")
    width = 1
    while width < count:
        value = value + lax.ppermute(value, "dp", [(r, r ^ width) for r in range(count)])
        width *= 2
    return value


def body(section_input, out_cotangent, up_weight, down_weight, norm_gain):
    section_count = lax.axis_size("section")
    section_pos = lax.axis_index("section")
    weight_up = up_weight[0]
    weight_down = down_weight[0]
    gain_row = norm_gain[0]
    model_width = weight_up.shape[0]
    inv_width = 1.0 / math.sqrt(D)
    inv_hidden = 1.0 / math.sqrt(HIDDEN_SIZE)
    first_chunk = section_input.reshape(-1, model_width)
    last_chunk = out_cotangent.reshape(-1, model_width)
    chunk_rows = first_chunk.shape[0]

    def keep(stash, fresh, section):
        return fresh if stash is None else jnp.where(section_pos == section, fresh, stash)

    rows_in = spread(first_chunk, 0, 0)
    grad_rows = spread(last_chunk, section_count - 1, section_count - 1)
    stash_rows = stash_scaled = stash_preact = stash_hidden = None
    for section in range(section_count):
        values, norm_scale, normed = normalize(rows_in)
        scaled = (normed * gain_row).astype(jnp.bfloat16)
        preact = jnp.dot(scaled, weight_up, preferred_element_type=jnp.float32) * inv_width
        hidden = gelu_value(preact).astype(jnp.bfloat16)
        stash_rows = keep(stash_rows, rows_in, section)
        stash_scaled = keep(stash_scaled, scaled, section)
        stash_preact = keep(stash_preact, preact, section)
        stash_hidden = keep(stash_hidden, hidden, section)
        if section < section_count - 1:
            part = (across_hidden(hidden, weight_down) * inv_hidden).astype(jnp.bfloat16)
            result = (values[:chunk_rows] + collect(part, section)).astype(jnp.bfloat16)
            rows_in = spread(result, section, section + 1)
    values, norm_scale, normed = normalize(stash_rows)
    own_scale, own_normed = norm_scale[:chunk_rows], normed[:chunk_rows]
    slope = gelu_slope(stash_preact)
    stash_grad = stash_preact_grad = gain_term = None
    for section in range(section_count - 1, -1, -1):
        hidden_grad = (
            jnp.dot(grad_rows, weight_down, preferred_element_type=jnp.float32) * inv_hidden
        )
        preact_grad = (hidden_grad * slope).astype(jnp.bfloat16)
        part = (across_hidden(preact_grad, weight_up) * inv_width).astype(jnp.bfloat16)
        stash_grad = keep(stash_grad, grad_rows, section)
        stash_preact_grad = keep(stash_preact_grad, preact_grad, section)
        if section > 0:
            scaled_grad = collect_all(part)
            gain_term = keep(gain_term, jnp.sum(scaled_grad * own_normed, axis=0), section)
            normed_grad = scaled_grad * gain_row
            input_grad = grad_rows[:chunk_rows].astype(jnp.float32) + own_scale * (
                normed_grad
                - own_normed * jnp.mean(normed_grad * own_normed, axis=-1, keepdims=True)
            )
            grad_rows = spread(input_grad.astype(jnp.bfloat16), section, section - 1)
        else:
            gain_term = keep(
                gain_term, jnp.sum(part.astype(jnp.float32) * normed, axis=0), section
            )
    grad_gain = sum_over_dp(gain_term)
    grad_down = outer_rows(stash_grad, stash_hidden) * inv_hidden
    grad_up = outer_rows(stash_scaled, stash_preact_grad) * inv_width
    return (grad_up[None], grad_down[None], grad_gain[None])


def solution(mesh):
    placed = (
        P(None, "dp", None),
        P(None, "dp", None),
        P("section", None, "dp"),
        P("section", None, "dp"),
        P("section", None),
    )
    return jax.shard_map(
        body,
        mesh=mesh,
        in_specs=placed,
        out_specs=(P("section", None, "dp"), P("section", None, "dp"), P("section", None)),
        check_vma=False,
    )
```

time: 1170 us -> 812 us (0.69)
  waiting for transfers between devices: 590 us -> 41.5 us
  starting transfers between devices: 14.9 us -> 422 us
  matrix products: 429 us -> 160 us
  local copies, waits for them, and re-layouts: 13.1 us -> 94.4 us
  between operations: 14.9 us -> 2.55 us
    psum x11 -> x0, waiting for transfers between devices: 586 us -> none  [the longest x5 332 us: body(): lax.psum(partial_value.astype(jnp.bfloat16), 'dp').astype(jnp.float32)]
    ppermute x10 -> x86, starting transfers between devices: 14.2 us -> 416 us  [the longest x83 405 us: send(): lax.ppermute(value, AXES, [(source * count + r, target * count + (r + ste...]
    dot_general x12 -> x2, matrix products: 230 us -> 25.5 us  [outer_rows(): lax.dot_general(left, right, (((0,), (0,)), ((), ())), preferred_element_...]
    concatenate x0 -> x8, local copies, waits for them, and re-layouts: none -> 72.6 us  [spread(): jnp.concatenate([send(chunk, source, target, k) for k in range(lax.axis_s...]
    all_gather x2 -> x0, blocking collectives: 66.5 us -> none  [the longest x1 34 us: body(): lax.all_gather(section_input, 'dp', axis=1, tiled=True)]
    all_to_all x0 -> x2, blocking collectives: none -> 55.5 us  [collect_all(): arrived = lax.all_to_all(placed, 'dp', 0, 0, tiled=True)]
    dot_general x11 -> x7, matrix products: 88.3 us -> 55.6 us  [across_hidden(): lax.dot_general(left, right, (((1,), (1,)), ((), ())), preferred_element_...]
    all_to_all x0 -> x1, waiting for transfers between devices: none -> 19.7 us  [collect_all(): arrived = lax.all_to_all(placed, 'dp', 0, 0, tiled=True)]
  transfers between devices with their start and end apart: 21 -> 87, of which waited for: 17 -> 13; matrix products, arithmetic and copies ran while one was open for 21% -> 4% of each run, Pallas kernels for 0% -> 0%
where the time goes in v1:
time: 812 us; the launch traced here: 801 us
  starting transfers between devices  422 us (52%)
  matrix products  160 us (20%)
  local copies, waits for them, and re-layouts  94.4 us (12%)
  blocking collectives  55.5 us (7%)
  waiting for transfers between devices  41.5 us (5%)
  other arithmetic  24.7 us (3%)
    ppermute x83, starting transfers between devices, send(): lax.ppermute(value, AXES, [(source * count + r, target * count + (r + ste...  405 us
    concatenate x8, local copies, waits for them, and re-layouts, spread(): jnp.concatenate([send(chunk, source, target, k) for k in range(lax.axis_s...  72.6 us
    dot_general x7, matrix products, across_hidden(): lax.dot_general(left, right, (((1,), (1,)), ((), ())), preferred_element_...  55.6 us
    all_to_all x2, blocking collectives, collect_all(): arrived = lax.all_to_all(placed, 'dp', 0, 0, tiled=True)  55.5 us
    dot_general x4, matrix products, body(): jnp.dot(scaled, weight_up, preferred_element_type=jnp.float32) * inv_width  39.4 us
    dot_general x4, matrix products, body(): jnp.dot(grad_rows, weight_down, preferred_element_type=jnp.float32)  39.2 us
    dot_general x2, matrix products, outer_rows(): lax.dot_general(left, right, (((0,), (0,)), ((), ())), preferred_element_...  25.5 us
    all_to_all x1, waiting for transfers between devices, collect_all(): arrived = lax.all_to_all(placed, 'dp', 0, 0, tiled=True)  19.7 us
  transfers between devices with their start and end apart: 87, of which 13 were waited for; matrix products, arithmetic and copies ran while one was open for 4% of the time, Pallas kernels for 0%

profile of v1, /device:TPU:0, one launch (start us, length us, event | category | flops | bytes accessed | tf_op | source)
XLA Modules:
  0.0 800.7 jit_solution(9990627137433434244)
XLA Ops:
  1.6 7.9 collective-permute-start.6
  35.9 9.7 %fusion.30 = f32[48,1120]{1,0:T(8,128)S(1)} fusion(bf16[1,6656,1120]{1,2,0:T(8,128)(2,1)} %param.7, f32[6656]{0:T(1024)S(1)} %reduce, f32[48]{0:T(128)S(1)} %add_rsqrt_fusion.4, bf16[48,6656]{1,0:T(8,128)(2,1)S(1)} %concatenate.39), kind=kOutput, calls=%fused_computation.32 | convolution fusion | flops 716931072 | bytes 15790272 | tf_op jit(solution)/shard_map/dot_general | solution.py:120
  45.5 7.9 fusion.59
  95.3 9.7 %fusion.28 = f32[48,1120]{1,0:T(8,128)S(1)} fusion(bf16[1,6656,1120]{1,2,0:T(8,128)(2,1)} %param.7, f32[48]{0:T(128)S(1)} %add_rsqrt_fusion.3, bf16[48,6656]{1,0:T(8,128)(2,1)S(1)} %concatenate.40, f32[6656]{0:T(1024)S(1)} %reduce), kind=kOutput, calls=%fused_computation.30 | convolution fusion | flops 716931072 | bytes 15790272 | tf_op jit(solution)/shard_map/dot_general | solution.py:120
  105.0 7.9 fusion.56
  118.1 27.1 %collective-permute-start.36 = (bf16[6,6656]{1,0:T(8,128)(2,1)S(1)}, bf16[6,6656]{1,0:T(8,128)(2,1)S(1)}, u32[]{:S(2)}, u32[]{:S(2)}) collective-permute-start(bf16[6,6656]{1,0:T(8,128)(2,1)S(1)} %fusion.170), channel_id=1, source_target_pairs={{8,23},{9,16},{10,17},{11,18},{12,19},{13,20},{14,21},{15,22}} | collective-permute-start | bytes 239624 | tf_op jit(solution)/shard_map/ppermute | solution.py:54
  160.7 11.8 %collective-permute-start.29 = (bf16[6,6656]{1,0:T(8,128)(2,1)S(1)}, bf16[6,6656]{1,0:T(8,128)(2,1)S(1)}, u32[]{:S(2)}, u32[]{:S(2)}) collective-permute-start(bf16[6,6656]{1,0:T(8,128)(2,1)S(1)} %fusion.170), channel_id=1, source_target_pairs={{8,16},{9,17},{10,18},{11,19},{12,20},{13,21},{14,22},{15,23}} | collective-permute-start | bytes 239624 | tf_op jit(solution)/shard_map/ppermute | solution.py:54
  174.2 9.7 %fusion.26 = f32[48,1120]{1,0:T(8,128)S(1)} fusion(bf16[1,6656,1120]{1,2,0:T(8,128)(2,1)} %param.7, f32[48]{0:T(128)S(1)} %add_rsqrt_fusion.2, bf16[48,6656]{1,0:T(8,128)(2,1)S(1)} %concatenate.41, f32[6656]{0:T(1024)S(1)} %reduce), kind=kOutput, calls=%fused_computation.28 | convolution fusion | flops 716931072 | bytes 15790272 | tf_op jit(solution)/shard_map/dot_general | solution.py:120
  183.9 7.9 fusion.53
  192.7 10.4 %collective-permute-start.37 = (bf16[6,6656]{1,0:T(8,128)(2,1)S(1)}, bf16[6,6656]{1,0:T(8,128)(2,1)S(1)}, u32[]{:S(2)}, u32[]{:S(2)}) collective-permute-start(bf16[6,6656]{1,0:T(8,128)(2,1)S(1)} %get-tuple-element.12), channel_id=1, source_target_pairs={{16,23},{17,16},{18,17},{19,18},{20,19},{21,20},{22,21},{23,22}} | collective-permute-start | bytes 239624 | tf_op jit(solution)/shard_map/ppermute | solution.py:54
  316.1 7.6 collective-permute-start.48
  357.3 10.1 %concatenate.42 = bf16[48,6656]{1,0:T(8,128)(2,1)S(1)} concatenate(bf16[6,6656]{1,0:T(8,128)(2,1)} %collective-permute-done.44, bf16[6,6656]{1,0:T(8,128)(2,1)} %collective-permute-done.45, bf16[6,6656]{1,0:T(8,128)(2,1)} %collective-permute-done.46, bf16[6,6656]{1,0:T(8,128)(2,1)} %collective-permute-done.47, bf16[6,6656]{1,0:T(8,128)(2,1)} %collective-permute-done.48, ...), dimensions={0} | concatenate | bytes 1277952 | tf_op jit(solution)/shard_map/concatenate | solution.py:62
  369.0 10.4 %fusion.163 = (f32[48,1120]{1,0:T(8,128)S(1)}, f32[48,1120]{1,0:T(8,128)}) fusion(f32[48,1120]{1,0:T(8,128)S(1)} %copy-done.11, f32[48,1120]{1,0:T(8,128)S(1)} %copy-done.8, f32[48,1120]{1,0:T(8,128)S(1)} %copy-done.5, pred[]{:T(512)S(6)} %eq.14, pred[]{:T(512)S(6)} %eq.12, pred[]{:T(512)S(6)} %eq.11, bf16[1,6656,1120]{1,2,0:T(8,128)(2,1)} %param.7, ...), kind=kOutput, calls=%fused_computation.139 | convolution fusion | flops 718221312 | bytes 16650435 | tf_op jit(solution)/shard_map/dot_general | solution.py:120
  379.4 9.6 %fusion.113 = bf16[48,1120]{1,0:T(8,128)(2,1)S(1)} fusion(f32[48,1120]{1,0:T(8,128)S(1)} %get-tuple-element.33, bf16[48,6656]{1,0:T(8,128)(2,1)S(1)} %concatenate.43, bf16[1,6656,1120]{1,2,0:T(8,128)(2,1)} %param.8), kind=kOutput, calls=%fused_computation.61 | convolution fusion | flops 715814400 | bytes 15870976 | tf_op jit(solution)/shard_map/dot_general | solution.py:136
  389.0 7.9 fusion.77
  414.3 19.7 %all-to-all-done = bf16[8,6,6656]{2,1,0:T(8,128)(2,1)} async-done(((bf16[8,6,6656]{2,1,0:T(8,128)(2,1)}), bf16[8,6,6656]{2,1,0:T(8,128)(2,1)}, u32[]{:S(2)}, u32[]{:S(2)}) %all-to-all-start) | async-done | bytes 639008 | tf_op jit(solution)/shard_map/all_to_all | solution.py:83
  486.5 7.8 collective-permute-start.59
  494.3 18.5 %concatenate.45 = bf16[48,6656]{1,0:T(8,128)(2,1)} concatenate(bf16[6,6656]{1,0:T(8,128)(2,1)} %collective-permute-done.59, bf16[6,6656]{1,0:T(8,128)(2,1)} %collective-permute-done.60, bf16[6,6656]{1,0:T(8,128)(2,1)} %collective-permute-done.61, bf16[6,6656]{1,0:T(8,128)(2,1)} %collective-permute-done.62, bf16[6,6656]{1,0:T(8,128)(2,1)} %collective-permute-done.63, ...), dimensions={0} | concatenate | bytes 1277952 | tf_op jit(solution)/shard_map/concatenate | solution.py:62
  512.8 9.8 %fusion.110 = bf16[48,1120]{1,0:T(8,128)(2,1)S(1)} fusion(f32[48,1120]{1,0:T(8,128)S(1)} %get-tuple-element.33, bf16[48,6656]{1,0:T(8,128)(2,1)} %concatenate.45, bf16[1,6656,1120]{1,2,0:T(8,128)(2,1)} %param.8), kind=kOutput, calls=%fused_computation.60 | convolution fusion | flops 715814400 | bytes 15870976 | tf_op jit(solution)/shard_map/dot_general | solution.py:136
  522.6 7.9 fusion.74
  538.3 28.2 %all_to_all.15 = bf16[8,6,6656]{2,1,0:T(8,128)(2,1)S(1)} all-to-all(bf16[8,6,6656]{2,1,0:T(8,128)(2,1)S(1)} %fusion.128), channel_id=1, replica_groups=mesh['section'=4,'dp'=8] {'dp'}, dimensions={0} | all-to-all | bytes 1277952 | tf_op jit(solution)/shard_map/all_to_all | solution.py:83
  612.3 7.6 collective-permute-start.68
  619.9 7.7 collective-permute-start.67
  627.6 18.4 %concatenate.47 = bf16[48,6656]{1,0:T(8,128)(2,1)} concatenate(bf16[6,6656]{1,0:T(8,128)(2,1)} %collective-permute-done.67, bf16[6,6656]{1,0:T(8,128)(2,1)} %collective-permute-done.68, bf16[6,6656]{1,0:T(8,128)(2,1)} %collective-permute-done.69, bf16[6,6656]{1,0:T(8,128)(2,1)} %collective-permute-done.70, bf16[6,6656]{1,0:T(8,128)(2,1)} %collective-permute-done.71, ...), dimensions={0} | concatenate | bytes 1277952 | tf_op jit(solution)/shard_map/concatenate | solution.py:62
  646.0 9.8 %fusion.107 = bf16[48,1120]{1,0:T(8,128)(2,1)S(1)} fusion(f32[48,1120]{1,0:T(8,128)S(1)} %get-tuple-element.33, bf16[48,6656]{1,0:T(8,128)(2,1)} %concatenate.47, bf16[1,6656,1120]{1,2,0:T(8,128)(2,1)} %param.8), kind=kOutput, calls=%fused_computation.59 | convolution fusion | flops 715814400 | bytes 15870976 | tf_op jit(solution)/shard_map/dot_general | solution.py:136
  655.9 7.9 fusion.71
  671.6 27.4 %all_to_all.16 = bf16[8,6,6656]{2,1,0:T(8,128)(2,1)S(1)} all-to-all(bf16[8,6,6656]{2,1,0:T(8,128)(2,1)S(1)} %fusion.125), channel_id=1, replica_groups=mesh['section'=4,'dp'=8] {'dp'}, dimensions={0} | all-to-all | bytes 1277952 | tf_op jit(solution)/shard_map/all_to_all | solution.py:83
  722.4 18.5 %concatenate.49 = bf16[48,6656]{1,0:T(8,128)(2,1)} concatenate(bf16[6,6656]{1,0:T(8,128)(2,1)} %collective-permute-done.75, bf16[6,6656]{1,0:T(8,128)(2,1)} %collective-permute-done.76, bf16[6,6656]{1,0:T(8,128)(2,1)} %collective-permute-done.77, bf16[6,6656]{1,0:T(8,128)(2,1)} %collective-permute-done.78, bf16[6,6656]{1,0:T(8,128)(2,1)} %collective-permute-done.79, ...), dimensions={0} | concatenate | bytes 1277952 | tf_op jit(solution)/shard_map/concatenate | solution.py:62
  740.8 9.9 %fusion.104 = bf16[48,1120]{1,0:T(8,128)(2,1)S(1)} fusion(f32[48,1120]{1,0:T(8,128)S(1)} %get-tuple-element.33, bf16[48,6656]{1,0:T(8,128)(2,1)} %concatenate.49, bf16[1,6656,1120]{1,2,0:T(8,128)(2,1)} %param.8), kind=kOutput, calls=%fused_computation.58 | convolution fusion | flops 715814400 | bytes 15870976 | tf_op jit(solution)/shard_map/dot_general | solution.py:136
  750.9 8.0 %fusion.120 = f32[6656]{0:T(1024)S(1)} fusion(bf16[48,1120]{1,0:T(8,128)(2,1)S(1)} %fusion.104, bf16[1,6656,1120]{1,2,0:T(8,128)(2,1)} %param.7, f32[48]{0:T(128)S(1)} %copy-done.31, bf16[48,6656]{1,0:T(8,128)(2,1)S(1)} %copy-done.3), kind=kOutput, calls=%fused_computation.91 | convolution fusion | flops 717882880 | bytes 15682752 | tf_op jit(solution)/shard_map/dot_general | solution.py:45
  768.5 12.7 %fusion = f32[1,6656,1120]{1,2,0:T(8,128)} fusion(pred[]{:T(512)S(6)} %eq.14, pred[]{:T(512)S(6)} %eq.12, pred[]{:T(512)S(6)} %eq.11, f32[6656]{0:T(1024)S(1)} %reduce, f32[48]{0:T(128)S(1)} %copy-done.35, bf16[48,6656]{1,0:T(8,128)(2,1)S(1)} %concatenate.39, f32[48]{0:T(128)S(1)} %copy-done.37, bf16[48,6656]{1,0:T(8,128)(2,1)S(1)} %concatenate.40, ...), kind=kOutput, calls=%fused_computation.2 | convolution fusion | flops 729339392 | bytes 32832260 | tf_op jit(solution)/shard_map/dot_general | solution.py:39
  787.1 12.8 %fusion.1 = f32[1,6656,1120]{1,2,0:T(8,128)} fusion(bf16[48,6656]{1,0:T(8,128)(2,1)S(1)} %copy-done.2, bf16[48,6656]{1,0:T(8,128)(2,1)S(1)} %copy-done.1, bf16[48,6656]{1,0:T(8,128)(2,1)S(1)} %copy-done, bf16[48,6656]{1,0:T(8,128)(2,1)S(1)} %concatenate.43, pred[]{:T(512)S(6)} %eq.15, pred[]{:T(512)S(6)} %eq.14, pred[]{:T(512)S(6)} %eq.12, ...), kind=kOutput, calls=%fused_computation.3 | convolution fusion | flops 726377984 | bytes 33234948 | tf_op jit(solution)/shard_map/dot_general | solution.py:39
  (303 shorter events, 409.9 us)
Async XLA Ops:
  118.1 41.2 %collective-permute-start.36 = (bf16[6,6656]{1,0:T(8,128)(2,1)S(1)}, bf16[6,6656]{1,0:T(8,128)(2,1)S(1)}, u32[]{:S(2)}, u32[]{:S(2)}) collective-permute-start(bf16[6,6656]{1,0:T(8,128)(2,1)S(1)} %fusion.170), channel_id=1, source_target_pairs={{8,23},{9,16},{10,17},{11,18},{12,19},{13,20},{14,21},{15,22}} | collective-permute-start | bytes 239624 | tf_op jit(solution)/shard_map/ppermute | solution.py:54
  192.7 39.1 %collective-permute-start.37 = (bf16[6,6656]{1,0:T(8,128)(2,1)S(1)}, bf16[6,6656]{1,0:T(8,128)(2,1)S(1)}, u32[]{:S(2)}, u32[]{:S(2)}) collective-permute-start(bf16[6,6656]{1,0:T(8,128)(2,1)S(1)} %get-tuple-element.12), channel_id=1, source_target_pairs={{16,23},{17,16},{18,17},{19,18},{20,19},{21,20},{22,21},{23,22}} | collective-permute-start | bytes 239624 | tf_op jit(solution)/shard_map/ppermute | solution.py:54
  203.1 35.7 %collective-permute-start.43 = (bf16[6,6656]{1,0:T(8,128)(2,1)S(1)}, bf16[6,6656]{1,0:T(8,128)(2,1)S(1)}, u32[]{:S(2)}, u32[]{:S(2)}) collective-permute-start(bf16[6,6656]{1,0:T(8,128)(2,1)S(1)} %get-tuple-element.13), channel_id=1, source_target_pairs={{16,17},{17,18},{18,19},{19,20},{20,21},{21,22},{22,23},{23,16}} | collective-permute-start | bytes 239624 | tf_op jit(solution)/shard_map/ppermute | solution.py:54
  210.1 36.8 %collective-permute-start.42 = (bf16[6,6656]{1,0:T(8,128)(2,1)S(1)}, bf16[6,6656]{1,0:T(8,128)(2,1)S(1)}, u32[]{:S(2)}, u32[]{:S(2)}) collective-permute-start(bf16[6,6656]{1,0:T(8,128)(2,1)S(1)} %get-tuple-element.14), channel_id=1, source_target_pairs={{16,18},{17,19},{18,20},{19,21},{20,22},{21,23},{22,16},{23,17}} | collective-permute-start | bytes 239624 | tf_op jit(solution)/shard_map/ppermute | solution.py:54
  217.1 36.2 %collective-permute-start.41 = (bf16[6,6656]{1,0:T(8,128)(2,1)S(1)}, bf16[6,6656]{1,0:T(8,128)(2,1)S(1)}, u32[]{:S(2)}, u32[]{:S(2)}) collective-permute-start(bf16[6,6656]{1,0:T(8,128)(2,1)S(1)} %get-tuple-element.15), channel_id=1, source_target_pairs={{16,19},{17,20},{18,21},{19,22},{20,23},{21,16},{22,17},{23,18}} | collective-permute-start | bytes 239624 | tf_op jit(solution)/shard_map/ppermute | solution.py:54
  224.1 35.9 %collective-permute-start.40 = (bf16[6,6656]{1,0:T(8,128)(2,1)S(1)}, bf16[6,6656]{1,0:T(8,128)(2,1)}, u32[]{:S(2)}, u32[]{:S(2)}) collective-permute-start(bf16[6,6656]{1,0:T(8,128)(2,1)S(1)} %get-tuple-element.16), channel_id=1, source_target_pairs={{16,20},{17,21},{18,22},{19,23},{20,16},{21,17},{22,18},{23,19}} | collective-permute-start | bytes 239624 | tf_op jit(solution)/shard_map/ppermute | solution.py:54
  231.8 35.1 %collective-permute-start.39 = (bf16[6,6656]{1,0:T(8,128)(2,1)}, bf16[6,6656]{1,0:T(8,128)(2,1)}, u32[]{:S(2)}, u32[]{:S(2)}) collective-permute-start(bf16[6,6656]{1,0:T(8,128)(2,1)} %get-tuple-element.17), channel_id=1, source_target_pairs={{16,21},{17,22},{18,23},{19,16},{20,17},{21,18},{22,19},{23,20}} | collective-permute-start | bytes 239624 | tf_op jit(solution)/shard_map/ppermute | solution.py:54
  238.8 34.8 %collective-permute-start.38 = (bf16[6,6656]{1,0:T(8,128)(2,1)S(1)}, bf16[6,6656]{1,0:T(8,128)(2,1)}, u32[]{:S(2)}, u32[]{:S(2)}) collective-permute-start(bf16[6,6656]{1,0:T(8,128)(2,1)S(1)} %get-tuple-element.18), channel_id=1, source_target_pairs={{16,22},{17,23},{18,16},{19,17},{20,18},{21,19},{22,20},{23,21}} | collective-permute-start | bytes 239624 | tf_op jit(solution)/shard_map/ppermute | solution.py:54
  246.9 34.8 %collective-permute-start.58 = (bf16[6,6656]{1,0:T(8,128)(2,1)S(1)}, bf16[6,6656]{1,0:T(8,128)(2,1)S(1)}, u32[]{:S(2)}, u32[]{:S(2)}) collective-permute-start(bf16[6,6656]{1,0:T(8,128)(2,1)S(1)} %reshape.140), channel_id=1, source_target_pairs={{24,31},{25,24},{26,25},{27,26},{28,27},{29,28},{30,29},{31,30}} | collective-permute-start | bytes 239624 | tf_op jit(solution)/shard_map/ppermute | solution.py:54
  253.3 35.2 %collective-permute-start.57 = (bf16[6,6656]{1,0:T(8,128)(2,1)S(1)}, bf16[6,6656]{1,0:T(8,128)(2,1)S(1)}, u32[]{:S(2)}, u32[]{:S(2)}) collective-permute-start(bf16[6,6656]{1,0:T(8,128)(2,1)S(1)} %reshape.140), channel_id=1, source_target_pairs={{24,30},{25,31},{26,24},{27,25},{28,26},{29,27},{30,28},{31,29}} | collective-permute-start | bytes 239624 | tf_op jit(solution)/shard_map/ppermute | solution.py:54
  260.1 35.2 %collective-permute-start.56 = (bf16[6,6656]{1,0:T(8,128)(2,1)S(1)}, bf16[6,6656]{1,0:T(8,128)(2,1)S(1)}, u32[]{:S(2)}, u32[]{:S(2)}) collective-permute-start(bf16[6,6656]{1,0:T(8,128)(2,1)S(1)} %reshape.140), channel_id=1, source_target_pairs={{24,29},{25,30},{26,31},{27,24},{28,25},{29,26},{30,27},{31,28}} | collective-permute-start | bytes 239624 | tf_op jit(solution)/shard_map/ppermute | solution.py:54
  266.9 35.2 %collective-permute-start.55 = (bf16[6,6656]{1,0:T(8,128)(2,1)S(1)}, bf16[6,6656]{1,0:T(8,128)(2,1)S(1)}, u32[]{:S(2)}, u32[]{:S(2)}) collective-permute-start(bf16[6,6656]{1,0:T(8,128)(2,1)S(1)} %reshape.140), channel_id=1, source_target_pairs={{24,28},{25,29},{26,30},{27,31},{28,24},{29,25},{30,26},{31,27}} | collective-permute-start | bytes 239624 | tf_op jit(solution)/shard_map/ppermute | solution.py:54
  273.7 35.4 %collective-permute-start.54 = (bf16[6,6656]{1,0:T(8,128)(2,1)S(1)}, bf16[6,6656]{1,0:T(8,128)(2,1)S(1)}, u32[]{:S(2)}, u32[]{:S(2)}) collective-permute-start(bf16[6,6656]{1,0:T(8,128)(2,1)S(1)} %reshape.140), channel_id=1, source_target_pairs={{24,27},{25,28},{26,29},{27,30},{28,31},{29,24},{30,25},{31,26}} | collective-permute-start | bytes 239624 | tf_op jit(solution)/shard_map/ppermute | solution.py:54
  281.7 34.4 %collective-permute-start.53 = (bf16[6,6656]{1,0:T(8,128)(2,1)S(1)}, bf16[6,6656]{1,0:T(8,128)(2,1)S(1)}, u32[]{:S(2)}, u32[]{:S(2)}) collective-permute-start(bf16[6,6656]{1,0:T(8,128)(2,1)S(1)} %reshape.140), channel_id=1, source_target_pairs={{24,26},{25,27},{26,28},{27,29},{28,30},{29,31},{30,24},{31,25}} | collective-permute-start | bytes 239624 | tf_op jit(solution)/shard_map/ppermute | solution.py:54
  288.5 35.3 %collective-permute-start.52 = (bf16[6,6656]{1,0:T(8,128)(2,1)S(1)}, bf16[6,6656]{1,0:T(8,128)(2,1)S(1)}, u32[]{:S(2)}, u32[]{:S(2)}) collective-permute-start(bf16[6,6656]{1,0:T(8,128)(2,1)S(1)} %reshape.140), channel_id=1, source_target_pairs={{24,25},{25,26},{26,27},{27,28},{28,29},{29,30},{30,31},{31,24}} | collective-permute-start | bytes 239624 | tf_op jit(solution)/shard_map/ppermute | solution.py:54
  295.3 36.1 %collective-permute-start.51 = (bf16[6,6656]{1,0:T(8,128)(2,1)S(1)}, bf16[6,6656]{1,0:T(8,128)(2,1)S(1)}, u32[]{:S(2)}, u32[]{:S(2)}) collective-permute-start(bf16[6,6656]{1,0:T(8,128)(2,1)S(1)} %fusion.169), channel_id=1, source_target_pairs={{16,31},{17,24},{18,25},{19,26},{20,27},{21,28},{22,29},{23,30}} | collective-permute-start | bytes 239624 | tf_op jit(solution)/shard_map/ppermute | solution.py:54
  302.0 37.0 %collective-permute-start.50 = (bf16[6,6656]{1,0:T(8,128)(2,1)S(1)}, bf16[6,6656]{1,0:T(8,128)(2,1)S(1)}, u32[]{:S(2)}, u32[]{:S(2)}) collective-permute-start(bf16[6,6656]{1,0:T(8,128)(2,1)S(1)} %fusion.169), channel_id=1, source_target_pairs={{16,30},{17,31},{18,24},{19,25},{20,26},{21,27},{22,28},{23,29}} | collective-permute-start | bytes 239624 | tf_op jit(solution)/shard_map/ppermute | solution.py:54
  309.1 37.6 %collective-permute-start.49 = (bf16[6,6656]{1,0:T(8,128)(2,1)S(1)}, bf16[6,6656]{1,0:T(8,128)(2,1)S(1)}, u32[]{:S(2)}, u32[]{:S(2)}) collective-permute-start(bf16[6,6656]{1,0:T(8,128)(2,1)S(1)} %fusion.169), channel_id=1, source_target_pairs={{16,29},{17,30},{18,31},{19,24},{20,25},{21,26},{22,27},{23,28}} | collective-permute-start | bytes 239624 | tf_op jit(solution)/shard_map/ppermute | solution.py:54
  316.1 41.2 %collective-permute-start.48 = (bf16[6,6656]{1,0:T(8,128)(2,1)S(1)}, bf16[6,6656]{1,0:T(8,128)(2,1)}, u32[]{:S(2)}, u32[]{:S(2)}) collective-permute-start(bf16[6,6656]{1,0:T(8,128)(2,1)S(1)} %fusion.169), channel_id=1, source_target_pairs={{16,28},{17,29},{18,30},{19,31},{20,24},{21,25},{22,26},{23,27}} | collective-permute-start | bytes 239624 | tf_op jit(solution)/shard_map/ppermute | solution.py:54
  323.7 33.5 %collective-permute-start.47 = (bf16[6,6656]{1,0:T(8,128)(2,1)S(1)}, bf16[6,6656]{1,0:T(8,128)(2,1)}, u32[]{:S(2)}, u32[]{:S(2)}) collective-permute-start(bf16[6,6656]{1,0:T(8,128)(2,1)S(1)} %fusion.169), channel_id=1, source_target_pairs={{16,27},{17,28},{18,29},{19,30},{20,31},{21,24},{22,25},{23,26}} | collective-permute-start | bytes 239624 | tf_op jit(solution)/shard_map/ppermute | solution.py:54
  331.4 25.9 %collective-permute-start.46 = (bf16[6,6656]{1,0:T(8,128)(2,1)S(1)}, bf16[6,6656]{1,0:T(8,128)(2,1)}, u32[]{:S(2)}, u32[]{:S(2)}) collective-permute-start(bf16[6,6656]{1,0:T(8,128)(2,1)S(1)} %fusion.169), channel_id=1, source_target_pairs={{16,26},{17,27},{18,28},{19,29},{20,30},{21,31},{22,24},{23,25}} | collective-permute-start | bytes 239624 | tf_op jit(solution)/shard_map/ppermute | solution.py:54
  406.1 27.9 %all-to-all-start = ((bf16[8,6,6656]{2,1,0:T(8,128)(2,1)}), bf16[8,6,6656]{2,1,0:T(8,128)(2,1)}, u32[]{:S(2)}, u32[]{:S(2)}) async-start(bf16[8,6,6656]{2,1,0:T(8,128)(2,1)} %fusion.131), calls=%async_computation | async-start | bytes 1703936 | tf_op jit(solution)/shard_map/all_to_all | solution.py:83
  438.0 33.6 %collective-permute-start.66 = (bf16[6,6656]{1,0:T(8,128)(2,1)S(1)}, bf16[6,6656]{1,0:T(8,128)(2,1)}, u32[]{:S(2)}, u32[]{:S(2)}) collective-permute-start(bf16[6,6656]{1,0:T(8,128)(2,1)S(1)} %add_convert_fusion.2), channel_id=1, source_target_pairs={{24,23},{25,16},{26,17},{27,18},{28,19},{29,20},{30,21},{31,22}} | collective-permute-start | bytes 239624 | tf_op jit(solution)/shard_map/ppermute | solution.py:54
  442.1 37.0 %collective-permute-start.65 = (bf16[6,6656]{1,0:T(8,128)(2,1)S(1)}, bf16[6,6656]{1,0:T(8,128)(2,1)}, u32[]{:S(2)}, u32[]{:S(2)}) collective-permute-start(bf16[6,6656]{1,0:T(8,128)(2,1)S(1)} %add_convert_fusion.2), channel_id=1, source_target_pairs={{24,22},{25,23},{26,16},{27,17},{28,18},{29,19},{30,20},{31,21}} | collective-permute-start | bytes 239624 | tf_op jit(solution)/shard_map/ppermute | solution.py:54
  449.5 37.0 %collective-permute-start.64 = (bf16[6,6656]{1,0:T(8,128)(2,1)S(1)}, bf16[6,6656]{1,0:T(8,128)(2,1)}, u32[]{:S(2)}, u32[]{:S(2)}) collective-permute-start(bf16[6,6656]{1,0:T(8,128)(2,1)S(1)} %add_convert_fusion.2), channel_id=1, source_target_pairs={{24,21},{25,22},{26,23},{27,16},{28,17},{29,18},{30,19},{31,20}} | collective-permute-start | bytes 239624 | tf_op jit(solution)/shard_map/ppermute | solution.py:54
  456.9 37.4 %collective-permute-start.63 = (bf16[6,6656]{1,0:T(8,128)(2,1)S(1)}, bf16[6,6656]{1,0:T(8,128)(2,1)}, u32[]{:S(2)}, u32[]{:S(2)}) collective-permute-start(bf16[6,6656]{1,0:T(8,128)(2,1)S(1)} %add_convert_fusion.2), channel_id=1, source_target_pairs={{24,20},{25,21},{26,22},{27,23},{28,16},{29,17},{30,18},{31,19}} | collective-permute-start | bytes 239624 | tf_op jit(solution)/shard_map/ppermute | solution.py:54
  464.3 30.0 %collective-permute-start.62 = (bf16[6,6656]{1,0:T(8,128)(2,1)S(1)}, bf16[6,6656]{1,0:T(8,128)(2,1)}, u32[]{:S(2)}, u32[]{:S(2)}) collective-permute-start(bf16[6,6656]{1,0:T(8,128)(2,1)S(1)} %add_convert_fusion.2), channel_id=1, source_target_pairs={{24,19},{25,20},{26,21},{27,22},{28,23},{29,16},{30,17},{31,18}} | collective-permute-start | bytes 239624 | tf_op jit(solution)/shard_map/ppermute | solution.py:54
  569.4 35.3 %collective-permute-start.74 = (bf16[6,6656]{1,0:T(8,128)(2,1)S(1)}, bf16[6,6656]{1,0:T(8,128)(2,1)}, u32[]{:S(2)}, u32[]{:S(2)}) collective-permute-start(bf16[6,6656]{1,0:T(8,128)(2,1)S(1)} %add_convert_fusion.1), channel_id=1, source_target_pairs={{16,15},{17,8},{18,9},{19,10},{20,11},{21,12},{22,13},{23,14}} | collective-permute-start | bytes 239624 | tf_op jit(solution)/shard_map/ppermute | solution.py:54
  574.1 38.2 %collective-permute-start.73 = (bf16[6,6656]{1,0:T(8,128)(2,1)S(1)}, bf16[6,6656]{1,0:T(8,128)(2,1)}, u32[]{:S(2)}, u32[]{:S(2)}) collective-permute-start(bf16[6,6656]{1,0:T(8,128)(2,1)S(1)} %add_convert_fusion.1), channel_id=1, source_target_pairs={{16,14},{17,15},{18,8},{19,9},{20,10},{21,11},{22,12},{23,13}} | collective-permute-start | bytes 239624 | tf_op jit(solution)/shard_map/ppermute | solution.py:54
  581.7 38.2 %collective-permute-start.72 = (bf16[6,6656]{1,0:T(8,128)(2,1)S(1)}, bf16[6,6656]{1,0:T(8,128)(2,1)}, u32[]{:S(2)}, u32[]{:S(2)}) collective-permute-start(bf16[6,6656]{1,0:T(8,128)(2,1)S(1)} %add_convert_fusion.1), channel_id=1, source_target_pairs={{16,13},{17,14},{18,15},{19,8},{20,9},{21,10},{22,11},{23,12}} | collective-permute-start | bytes 239624 | tf_op jit(solution)/shard_map/ppermute | solution.py:54
  589.4 38.2 %collective-permute-start.71 = (bf16[6,6656]{1,0:T(8,128)(2,1)S(1)}, bf16[6,6656]{1,0:T(8,128)(2,1)}, u32[]{:S(2)}, u32[]{:S(2)}) collective-permute-start(bf16[6,6656]{1,0:T(8,128)(2,1)S(1)} %add_convert_fusion.1), channel_id=1, source_target_pairs={{16,12},{17,13},{18,14},{19,15},{20,8},{21,9},{22,10},{23,11}} | collective-permute-start | bytes 239624 | tf_op jit(solution)/shard_map/ppermute | solution.py:54
  597.0 30.6 %collective-permute-start.70 = (bf16[6,6656]{1,0:T(8,128)(2,1)S(1)}, bf16[6,6656]{1,0:T(8,128)(2,1)}, u32[]{:S(2)}, u32[]{:S(2)}) collective-permute-start(bf16[6,6656]{1,0:T(8,128)(2,1)S(1)} %add_convert_fusion.1), channel_id=1, source_target_pairs={{16,11},{17,12},{18,13},{19,14},{20,15},{21,8},{22,9},{23,10}} | collective-permute-start | bytes 239624 | tf_op jit(solution)/shard_map/ppermute | solution.py:54
  (95 other events, 1235.8 us)

commit v2 on v1

v2 whole, which is shorter than its diff:
```python
import functools
import math

import jax
import jax.numpy as jnp
from jax import lax
from jax.experimental import pallas as pl
from jax.experimental.pallas import tpu as pltpu
from jax.sharding import PartitionSpec as P

D = 6656
HIDDEN_SIZE = 8960


EPSILON = 1e-05
GELU_SCALE = 0.7978845608028654
GELU_CUBIC = 0.044715

INV_WIDTH = 1.0 / math.sqrt(D)
INV_HIDDEN = 1.0 / math.sqrt(HIDDEN_SIZE)

AXES = ("section", "dp")
QUARTERS = 4
LANES = 128
BLOCK = 512
VMEM_BYTES = 50 * 1024 * 1024

ANY = pl.BlockSpec(memory_space=pl.ANY)
VMEM = pl.BlockSpec(memory_space=pltpu.VMEM)
SMEM = pl.BlockSpec(memory_space=pltpu.SMEM)


def gelu_value(preact):
    inner = GELU_SCALE * (preact + GELU_CUBIC * preact * preact * preact)
    return 0.5 * preact * (1.0 + jnp.tanh(inner))


def gelu_slope(preact):
    inner = GELU_SCALE * (preact + GELU_CUBIC * preact * preact * preact)
    tangent = jnp.tanh(inner)
    return 0.5 * (1.0 + tangent) + 0.5 * preact * (1.0 - tangent * tangent) * GELU_SCALE * (
        1.0 + 3.0 * GELU_CUBIC * preact * preact
    )


def outer_rows(left, right):
    return lax.dot_general(
        left, right, (((0,), (0,)), ((), ())), preferred_element_type=jnp.float32
    )


def across_hidden(left, right):
    return lax.dot_general(
        left, right, (((1,), (1,)), ((), ())), preferred_element_type=jnp.float32
    )


def block_copies(source, target, sems):
    return [
        pltpu.make_async_copy(
            source.at[pl.ds(i * BLOCK, BLOCK)], target.at[pl.ds(i * BLOCK, BLOCK)], sems.at[i]
        )
        for i in range(source.shape[0] // BLOCK)
    ]


def quarter(place_ref, k, width):
    start = (place_ref[1] ^ k) * width
    return pl.ds(pl.multiple_of(start, LANES), width)


def contract_width(rows_ref, weight_ref, total_ref, copies, then_start):
    for i, copy in enumerate(copies):
        if i < len(then_start):
            then_start[i].start()
        copy.wait()
        part = jnp.dot(
            rows_ref[:, i * BLOCK : (i + 1) * BLOCK],
            weight_ref[i * BLOCK : (i + 1) * BLOCK, :],
            preferred_element_type=jnp.float32,
        )
        total_ref[...] = part if i == 0 else total_ref[...] + part


def forward_kernel(pieces, with_down, with_stash, *refs):
    place_ref, refs = refs[0], refs[1:]
    piece_refs, refs = refs[:pieces], refs[pieces:]
    gain_ref, up_hbm, down_hbm = refs[:3]
    refs = refs[3 + (3 if with_stash else 0) :]
    count = QUARTERS if with_down else 0
    part_refs, refs = refs[:count], refs[count:]
    rows_out, scale_out, preact_out = refs[:3]
    up_ref, down_ref, rows_ref, scaled_ref, scale_ref, preact_ref, part_ref = refs[3:10]
    up_sems, down_sems, out_sems = refs[10:]
    width = rows_ref.shape[1]
    piece_width = width // pieces

    @pl.when(place_ref[0] == 1)
    def _():
        up_copies = block_copies(up_hbm, up_ref, up_sems)
        down_copies = block_copies(down_hbm, down_ref, down_sems) if with_down else []
        for copy in up_copies:
            copy.start()
        squares = 0.0
        for k in range(pieces):
            values = piece_refs[k][...].astype(jnp.float32)
            squares = squares + jnp.sum(values * values, axis=-1, keepdims=True)
        norm_scale = lax.rsqrt(squares * (1.0 / width) + EPSILON)
        scale_ref[...] = jnp.broadcast_to(norm_scale, scale_ref.shape)
        for k in range(pieces):
            columns = quarter(place_ref, k, piece_width) if pieces > 1 else slice(None)
            rows = piece_refs[k][...]
            rows_ref[:, columns] = rows
            normed = rows.astype(jnp.float32) * norm_scale
            scaled_ref[:, columns] = (normed * gain_ref[:, columns]).astype(jnp.bfloat16)
        contract_width(scaled_ref, up_ref, preact_ref, up_copies, down_copies)
        preact = preact_ref[...] * INV_WIDTH
        preact_ref[...] = preact
        stores = [
            pltpu.make_async_copy(source, target, out_sems.at[i])
            for i, (source, target) in enumerate(
                [(rows_ref, rows_out), (scale_ref, scale_out), (preact_ref, preact_out)]
            )
        ]
        for copy in stores:
            copy.start()
        if with_down:
            hidden = gelu_value(preact).astype(jnp.bfloat16)
            for i, copy in enumerate(down_copies):
                copy.wait()
                block = slice(i * BLOCK, (i + 1) * BLOCK)
                part = across_hidden(hidden, down_ref[block, :]) * INV_HIDDEN
                part_ref[:, block] = part.astype(jnp.bfloat16)
            for k in range(QUARTERS):
                part_refs[k][...] = part_ref[:, quarter(place_ref, k, width // QUARTERS)]
        for copy in stores:
            copy.wait()


def backward_kernel(pieces, with_parts, with_stash, *refs):
    place_ref, refs = refs[0], refs[1:]
    piece_refs, refs = refs[:pieces], refs[pieces:]
    rows_ref, scale_ref, preact_ref, up_hbm, down_hbm = refs[:5]
    refs = refs[5 + (3 if with_stash else 0) :]
    count = QUARTERS if with_parts else 0
    part_refs, refs = refs[:count], refs[count:]
    grad_out, preact_grad_out, gain_out = refs[:3]
    up_ref, down_ref, grad_ref, hidden_grad_ref, preact_grad_ref, part_ref, gain_ref = refs[3:10]
    up_sems, down_sems, out_sems = refs[10:]
    width = grad_ref.shape[1]
    piece_width = width // pieces

    @pl.when(place_ref[0] == 1)
    def _():
        up_copies = block_copies(up_hbm, up_ref, up_sems)
        down_copies = block_copies(down_hbm, down_ref, down_sems)
        for copy in down_copies:
            copy.start()
        for k in range(pieces):
            columns = quarter(place_ref, k, piece_width) if pieces > 1 else slice(None)
            grad_ref[:, columns] = piece_refs[k][...]
        contract_width(grad_ref, down_ref, hidden_grad_ref, down_copies, up_copies)
        preact = preact_ref[...]
        hidden_grad = hidden_grad_ref[...] * INV_HIDDEN
        preact_grad = (hidden_grad * gelu_slope(preact)).astype(jnp.bfloat16)
        preact_grad_ref[...] = preact_grad
        norm_scale = scale_ref[:, :1]
        for i, copy in enumerate(up_copies):
            copy.wait()
            block = slice(i * BLOCK, (i + 1) * BLOCK)
            part = across_hidden(preact_grad, up_ref[block, :]) * INV_WIDTH
            normed = rows_ref[:, block].astype(jnp.float32) * norm_scale
            gain_ref[:, block] = jnp.sum(part * normed, axis=0, keepdims=True)
            if with_parts:
                part_ref[:, block] = part.astype(jnp.bfloat16)
        stores = [
            pltpu.make_async_copy(source, target, out_sems.at[i])
            for i, (source, target) in enumerate(
                [
                    (grad_ref, grad_out),
                    (preact_grad_ref, preact_grad_out),
                    (gain_ref, gain_out),
                ]
            )
        ]
        for copy in stores:
            copy.start()
        if with_parts:
            along = jnp.sum(
                preact_grad.astype(jnp.float32) * preact, axis=-1, keepdims=True
            ).astype(jnp.bfloat16)
            quarter_width = width // QUARTERS
            for k in range(QUARTERS):
                part_refs[k][:, :quarter_width] = part_ref[
                    :, quarter(place_ref, k, quarter_width)
                ]
                part_refs[k][:, quarter_width:] = jnp.broadcast_to(along, (along.shape[0], LANES))
        for copy in stores:
            copy.wait()


def call(kernel, inputs, specs, stash, parts, stash_shapes, scratch, passes, shapes):
    rows, width, local = shapes
    aliases = {len(inputs) + i: len(parts) + i for i in range(len(stash))}
    bytes_accessed = passes * width * local * 2
    return pl.pallas_call(
        kernel,
        out_shape=list(parts) + list(stash_shapes),
        in_specs=list(specs) + [ANY] * len(stash),
        out_specs=[VMEM] * len(parts) + [ANY] * len(stash_shapes),
        scratch_shapes=scratch,
        input_output_aliases=aliases,
        cost_estimate=pl.CostEstimate(
            flops=passes * 2 * rows * width * local,
            bytes_accessed=bytes_accessed,
            transcendentals=rows * local,
        ),
        compiler_params=pltpu.CompilerParams(vmem_limit_bytes=VMEM_BYTES),
    )(*inputs, *stash)


def forward_stage(place, pieces, gain, up, down, stash, with_down):
    rows = pieces[0].shape[0]
    width, local = up.shape
    blocks = width // BLOCK
    parts = [jax.ShapeDtypeStruct((rows, width // QUARTERS), jnp.bfloat16)] * QUARTERS
    stash_shapes = [
        jax.ShapeDtypeStruct((rows, width), jnp.bfloat16),
        jax.ShapeDtypeStruct((rows, LANES), jnp.float32),
        jax.ShapeDtypeStruct((rows, local), jnp.float32),
    ]
    scratch = [
        pltpu.VMEM((width, local), jnp.bfloat16),
        pltpu.VMEM((width, local) if with_down else (16, LANES), jnp.bfloat16),
        pltpu.VMEM((rows, width), jnp.bfloat16),
        pltpu.VMEM((rows, width), jnp.bfloat16),
        pltpu.VMEM((rows, LANES), jnp.float32),
        pltpu.VMEM((rows, local), jnp.float32),
        pltpu.VMEM((rows, width), jnp.bfloat16),
        pltpu.SemaphoreType.DMA((blocks,)),
        pltpu.SemaphoreType.DMA((blocks,)),
        pltpu.SemaphoreType.DMA((3,)),
    ]
    result = call(
        functools.partial(forward_kernel, len(pieces), with_down, bool(stash)),
        [place, *pieces, gain, up, down],
        [SMEM] + [VMEM] * len(pieces) + [VMEM, ANY, ANY],
        stash,
        parts if with_down else [],
        stash_shapes,
        scratch,
        2 if with_down else 1,
        (rows, width, local),
    )
    return (result[:-3], result[-3:])


def backward_stage(place, pieces, kept, up, down, stash, with_parts):
    rows = pieces[0].shape[0]
    width, local = up.shape
    blocks = width // BLOCK
    parts = [jax.ShapeDtypeStruct((rows, width // QUARTERS + LANES), jnp.bfloat16)] * QUARTERS
    stash_shapes = [
        jax.ShapeDtypeStruct((rows, width), jnp.bfloat16),
        jax.ShapeDtypeStruct((rows, local), jnp.bfloat16),
        jax.ShapeDtypeStruct((1, width), jnp.float32),
    ]
    scratch = [
        pltpu.VMEM((width, local), jnp.bfloat16),
        pltpu.VMEM((width, local), jnp.bfloat16),
        pltpu.VMEM((rows, width), jnp.bfloat16),
        pltpu.VMEM((rows, local), jnp.float32),
        pltpu.VMEM((rows, local), jnp.bfloat16),
        pltpu.VMEM((rows, width), jnp.bfloat16),
        pltpu.VMEM((1, width), jnp.float32),
        pltpu.SemaphoreType.DMA((blocks,)),
        pltpu.SemaphoreType.DMA((blocks,)),
        pltpu.SemaphoreType.DMA((3,)),
    ]
    result = call(
        functools.partial(backward_kernel, len(pieces), with_parts, bool(stash)),
        [place, *pieces, *kept, up, down],
        [SMEM] + [VMEM] * (len(pieces) + 3) + [ANY, ANY],
        stash,
        parts if with_parts else [],
        stash_shapes,
        scratch,
        2,
        (rows, width, local),
    )
    return (result[:-3], result[-3:])


def within(sections, flip):
    count = lax.axis_size("dp")
    return [(s * count + r, s * count + (r ^ flip)) for s in sections for r in range(count)]


def between(moves, flip):
    count = lax.axis_size("dp")
    return [(s * count + r, t * count + (r ^ flip)) for s, t in moves for r in range(count)]


def sum_quarters(parts, sections):
    inner = lax.axis_size("dp") // QUARTERS
    total = parts[0].astype(jnp.float32)
    arrived = [
        lax.ppermute(parts[k], AXES, within(sections, k * inner)) for k in range(QUARTERS - 1, 0, -1)
    ]
    for value in arrived:
        total = total + value.astype(jnp.float32)
    flip = 1
    while flip < inner:
        rounded = total.astype(jnp.bfloat16)
        other = lax.ppermute(rounded, AXES, within(sections, flip))
        total = rounded.astype(jnp.float32) + other.astype(jnp.float32)
        flip *= 2
    return total


def hand_on(own, moves):
    inner = lax.axis_size("dp") // QUARTERS
    pieces = {
        k: lax.ppermute(own, AXES, between(moves, k * inner)) for k in range(QUARTERS - 1, -1, -1)
    }
    return [pieces[k] for k in range(QUARTERS)]


def gather_rows(chunk, sections):
    count = lax.axis_size("dp")
    position = lax.axis_index("dp")
    held = chunk[None]
    flip = 1
    while flip < count:
        other = lax.ppermute(held, AXES, within(sections, flip))
        low = (position // flip) % 2 == 0
        held = jnp.concatenate([jnp.where(low, held, other), jnp.where(low, other, held)], axis=0)
        flip *= 2
    return held.reshape(-1, chunk.shape[-1])


def sum_over_dp(value):
    flip = 1
    while flip < lax.axis_size("dp"):
        value = value + lax.ppermute(
            value, "dp", [(r, r ^ flip) for r in range(lax.axis_size("dp"))]
        )
        flip *= 2
    return value


def body(section_input, out_cotangent, up_weight, down_weight, norm_gain):
    section_count = lax.axis_size("section")
    section_pos = lax.axis_index("section")
    inner = lax.axis_size("dp") // QUARTERS
    outer_pos = lax.axis_index("dp") // inner
    weight_up = up_weight[0]
    weight_down = down_weight[0]
    width = weight_up.shape[0]
    quarter_width = width // QUARTERS
    last = section_count - 1

    def place(section):
        return jnp.stack([section_pos == section, outer_pos]).astype(jnp.int32)

    def alike(section):
        return [s for s in range(section_count) if s % 2 == section % 2]

    def moves(section, step):
        return [(s, s + step) for s in alike(section) if 0 <= s + step < section_count]

    chunk = jnp.where(section_pos == last, out_cotangent, section_input)
    entered = gather_rows(chunk.reshape(-1, width), [0, last])

    pieces, stash = [entered], ()
    for section in range(section_count):
        parts, stash = forward_stage(
            place(section), pieces, norm_gain, weight_up, weight_down, stash, section < last
        )
        if section < last:
            if section == 0:
                own = lax.dynamic_slice_in_dim(entered, outer_pos * quarter_width, quarter_width, 1)
            else:
                own = pieces[0]
            result = own.astype(jnp.float32) + sum_quarters(parts, alike(section))
            pieces = hand_on(result.astype(jnp.bfloat16), moves(section, 1))

    rows, scale, preact = stash
    own_scale = scale[:, :1]
    own_rows = lax.dynamic_slice_in_dim(rows, outer_pos * quarter_width, quarter_width, 1)
    own_normed = own_rows.astype(jnp.float32) * own_scale
    own_gain = lax.dynamic_slice_in_dim(norm_gain, outer_pos * quarter_width, quarter_width, 1)
    pieces, grads = [entered], ()
    for section in range(last, -1, -1):
        parts, grads = backward_stage(
            place(section), pieces, stash, weight_up, weight_down, grads, section > 0
        )
        if section > 0:
            if section == last:
                own = lax.dynamic_slice_in_dim(entered, outer_pos * quarter_width, quarter_width, 1)
            else:
                own = pieces[0]
            total = sum_quarters(parts, alike(section))
            along = total[:, quarter_width : quarter_width + 1] * (1.0 / width)
            normed_grad = total[:, :quarter_width] * own_gain
            result = own.astype(jnp.float32) + own_scale * (normed_grad - own_normed * along)
            pieces = hand_on(result.astype(jnp.bfloat16), moves(section, -1))

    grad_rows, preact_grad, gain_part = grads
    grad_gain = sum_over_dp(gain_part)
    normed = rows.astype(jnp.float32) * own_scale
    scaled = (normed * norm_gain).astype(jnp.bfloat16)
    hidden = gelu_value(preact).astype(jnp.bfloat16)
    grad_down = outer_rows(grad_rows, hidden) * INV_HIDDEN
    grad_up = outer_rows(scaled, preact_grad) * INV_WIDTH
    return (grad_up[None], grad_down[None], grad_gain)


def solution(mesh):
    placed = (
        P(None, "dp", None),
        P(None, "dp", None),
        P("section", None, "dp"),
        P("section", None, "dp"),
        P("section", None),
    )
    return jax.shard_map(
        body,
        mesh=mesh,
        in_specs=placed,
        out_specs=(P("section", None, "dp"), P("section", None, "dp"), P("section", None)),
        check_vma=False,
    )
```

time: 812 us -> 404 us (0.50)
  starting transfers between devices: 422 us -> 115 us
  matrix products: 160 us -> 25.2 us
  waiting for transfers between devices: 41.5 us -> 175 us
  blocking collectives: 55.5 us -> 0 us
  local copies, waits for them, and re-layouts: 94.4 us -> 42.6 us
  Pallas kernels: 0 us -> 32.5 us
  other arithmetic: 24.7 us -> 4.21 us
    ppermute x86 -> x54, starting transfers between devices: 416 us -> 115 us  [the longest x24 48 us: hand_on(): lax.ppermute(own, AXES, between(moves, k * inner))]
    ppermute x86 -> x54, waiting for transfers between devices: 21.8 us -> 175 us  [the longest x24 140 us: hand_on(): lax.ppermute(own, AXES, between(moves, k * inner))]
    dot_general x15 -> x0, matrix products: 134 us -> none  [the longest x7 55.6 us: across_hidden(): lax.dot_general(left, right, (((1,), (1,)), ((), ())), preferred_element_...]
    concatenate x8 -> x0, local copies, waits for them, and re-layouts: 72.6 us -> none  [spread(): jnp.concatenate([send(chunk, source, target, k) for k in range(lax.axis_s...]
    all_to_all x2 -> x0, blocking collectives: 55.5 us -> none  [collect_all(): arrived = lax.all_to_all(placed, 'dp', 0, 0, tiled=True)]
    unnamed x80 -> x4, local copies, waits for them, and re-layouts: 0.68 us -> 42.2 us
    pallas_call x0 -> x8, Pallas kernels: none -> 32.5 us  [call(): pl.pallas_call(kernel, out_shape=list(parts) + list(stash_shapes), in_spe...]
    all_to_all x1 -> x0, waiting for transfers between devices: 19.7 us -> none  [collect_all(): arrived = lax.all_to_all(placed, 'dp', 0, 0, tiled=True)]
  transfers between devices with their start and end apart: 87 -> 54, of which waited for: 13 -> 22; matrix products, arithmetic and copies ran while one was open for 4% -> 17% of each run, Pallas kernels for 0% -> 0%
where the time goes in v2:
time: 404 us; the launch traced here: 397 us
  waiting for transfers between devices  175 us (43%)
  starting transfers between devices  115 us (28%)
  local copies, waits for them, and re-layouts  42.6 us (11%)
  Pallas kernels  32.5 us (8%)
  matrix products  25.2 us (6%)
  other arithmetic  4.21 us (1%)
    ppermute x24, waiting for transfers between devices, hand_on(): lax.ppermute(own, AXES, between(moves, k * inner))  140 us
    ppermute x24, starting transfers between devices, hand_on(): lax.ppermute(own, AXES, between(moves, k * inner))  48 us
    unnamed x4, local copies, waits for them, and re-layouts  42.2 us
    ppermute x18, starting transfers between devices, sum_quarters(): lax.ppermute(parts[k], AXES, within(sections, k * inner))  36.4 us
    pallas_call x8, Pallas kernels, call(): pl.pallas_call(kernel, out_shape=list(parts) + list(stash_shapes), in_spe...  32.5 us
    dot_general x2, matrix products, outer_rows(): lax.dot_general(left, right, (((0,), (0,)), ((), ())), preferred_element_...  25.2 us
    ppermute x18, waiting for transfers between devices, sum_quarters(): lax.ppermute(parts[k], AXES, within(sections, k * inner))  15.7 us
    ppermute x3, starting transfers between devices, gather_rows(): other = lax.ppermute(held, AXES, within(sections, flip))  13.8 us
  transfers between devices with their start and end apart: 54, of which 22 were waited for; matrix products, arithmetic and copies ran while one was open for 17% of the time, Pallas kernels for 0%

profile of v2, /device:TPU:0, one launch (start us, length us, event | category | flops | bytes accessed | tf_op | source)
XLA Modules:
  0.0 396.7 jit_solution(3409319086508615997)
XLA Ops:
  1.7 4.9 %collective-permute-start = (bf16[1,6,6656]{2,1,0:T(8,128)(2,1)S(1)}, bf16[1,6,6656]{2,1,0:T(8,128)(2,1)S(1)}, u32[]{:S(2)}, u32[]{:S(2)}) collective-permute-start(bf16[1,6,6656]{2,1,0:T(8,128)(2,1)S(1)} %broadcast_in_dim_reshape.3), channel_id=1, source_target_pairs={{0,1},{1,0},{2,3},{3,2},{4,5},{5,4},{6,7},{7,6},{24,25},{25,24},{2... | collective-permute-start | bytes 239624 | tf_op jit(solution)/shard_map/ppermute | solution.py:335
  9.3 4.0 %collective-permute-start.1 = (bf16[2,6,6656]{2,1,0:T(8,128)(2,1)S(1)}, bf16[2,6,6656]{2,1,0:T(8,128)(2,1)S(1)}, u32[]{:S(2)}, u32[]{:S(2)}) collective-permute-start(bf16[2,6,6656]{2,1,0:T(8,128)(2,1)S(1)} %pad_maximum_fusion.2), channel_id=1, source_target_pairs={{0,2},{1,3},{2,0},{3,1},{4,6},{5,7},{6,4},{7,5},{24,26},{25,27},{2... | collective-permute-start | bytes 479240 | tf_op jit(solution)/shard_map/ppermute | solution.py:335
  13.3 3.8 collective-permute-done.1
  17.3 4.9 %collective-permute-start.2 = (bf16[4,6,6656]{2,1,0:T(8,128)(2,1)S(1)}, bf16[4,6,6656]{2,1,0:T(8,128)(2,1)S(1)}, u32[]{:S(2)}, u32[]{:S(2)}) collective-permute-start(bf16[4,6,6656]{2,1,0:T(8,128)(2,1)S(1)} %pad_maximum_fusion.1), channel_id=1, source_target_pairs={{0,4},{1,5},{2,6},{3,7},{4,0},{5,1},{6,2},{7,3},{24,28},{25,29},{2... | collective-permute-start | bytes 958472 | tf_op jit(solution)/shard_map/ppermute | solution.py:335
  22.2 21.1 %copy.28 = bf16[1,6656,1120]{2,1,0:T(8,128)(2,1)} copy(bf16[1,6656,1120]{1,2,0:T(8,128)(2,1)} %param.7) | data formatting | bytes 29818880 | tf_op args[2]
  43.3 21.1 %copy.29 = bf16[1,6656,1120]{2,1,0:T(8,128)(2,1)} copy(bf16[1,6656,1120]{1,2,0:T(8,128)(2,1)} %param.8) | data formatting | bytes 29818880 | tf_op args[3]
  65.1 13.3 %shard_map.76 = (bf16[48,1664]{1,0:T(8,128)(2,1)S(1)}, bf16[48,1664]{1,0:T(8,128)(2,1)S(1)}, bf16[48,1664]{1,0:T(8,128)(2,1)S(1)}, bf16[48,1664]{1,0:T(8,128)(2,...) custom-call(s32[2]{0:T(128)S(1)} %pad_add_fusion.1.refs_0_, ...), custom_call_target="tpu_custom_call" | custom-call | flops 1431306240 | bytes 29818880 | tf_op jit(solution)/shard_map/pallas_call | solution.py:206
  78.4 3.3 collective-permute-start.3
  81.7 3.6 collective-permute-start.4
  88.5 3.3 collective-permute-done.4
  93.5 3.4 collective-permute-start.6
  97.0 3.7 collective-permute-done.6
  117.1 3.3 collective-permute-start.19
  122.9 4.3 %collective-permute-start.21 = (bf16[48,1664]{1,0:T(8,128)(2,1)S(1)}, bf16[48,1664]{1,0:T(8,128)(2,1)S(1)}, u32[]{:S(2)}, u32[]{:S(2)}) collective-permute-start(bf16[48,1664]{1,0:T(8,128)(2,1)S(1)} %get-tuple-element.68), channel_id=1, source_target_pairs={{0,2},{1,3},{2,0},{3,1},{4,6},{5,7},{6,4},{7,5},{16,18},{17,19},{1... | collective-permute-start | bytes 479240 | tf_op jit(solution)/shard_map/ppermute | solution.py:308
  127.2 3.5 collective-permute-done.20
  132.4 3.4 collective-permute-start.22
  135.8 3.7 collective-permute-done.22
  139.6 19.3 %collective-permute-start.23 = (bf16[48,1664]{1,0:T(8,128)(2,1)S(1)}, bf16[48,1664]{1,0:T(8,128)(2,1)S(1)}, u32[]{:S(2)}, u32[]{:S(2)}) collective-permute-start(bf16[48,1664]{1,0:T(8,128)(2,1)S(1)} %add_convert_fusion.3), channel_id=1, source_target_pairs={{0,8},{1,9},{2,10},{3,11},{4,12},{5,13},{6,14},{7,15},{16,24},{17,... | collective-permute-start | bytes 479240 | tf_op jit(solution)/shard_map/ppermute | solution.py:324
  159.0 4.2 %collective-permute-start.24 = (bf16[48,1664]{1,0:T(8,128)(2,1)S(1)}, bf16[48,1664]{1,0:T(8,128)(2,1)S(1)}, u32[]{:S(2)}, u32[]{:S(2)}) collective-permute-start(bf16[48,1664]{1,0:T(8,128)(2,1)S(1)} %add_convert_fusion.3), channel_id=1, source_target_pairs={{0,10},{1,11},{2,8},{3,9},{4,14},{5,15},{6,12},{7,13},{16,26},{17,... | collective-permute-start | bytes 479240 | tf_op jit(solution)/shard_map/ppermute | solution.py:324
  180.2 17.6 %collective-permute-done.31.refs_1_ = bf16[48,1664]{1,0:T(8,128)(2,1)S(1)} collective-permute-done((bf16[48,1664]{1,0:T(8,128)(2,1)S(1)}, bf16[48,1664]{1,0:T(8,128)(2,1)S(1)}, u32[]{:S(2)}, u32[]{:S(2)}) %collective-permute-start.31) | collective-permute-done | bytes 159776 | tf_op jit(solution)/shard_map/ppermute | solution.py:324
  197.8 4.5 %collective-permute-done.32.refs_2_ = bf16[48,1664]{1,0:T(8,128)(2,1)S(1)} collective-permute-done((bf16[48,1664]{1,0:T(8,128)(2,1)S(1)}, bf16[48,1664]{1,0:T(8,128)(2,1)S(1)}, u32[]{:S(2)}, u32[]{:S(2)}) %collective-permute-start.32) | collective-permute-done | bytes 159776 | tf_op jit(solution)/shard_map/ppermute | solution.py:324
  202.3 3.5 collective-permute-done.34.refs_4_
  206.9 4.2 %collective-permute-start.35 = (bf16[48,1792]{1,0:T(8,128)(2,1)S(1)}, bf16[48,1792]{1,0:T(8,128)(2,1)S(1)}, u32[]{:S(2)}, u32[]{:S(2)}) collective-permute-start(bf16[48,1792]{1,0:T(8,128)(2,1)S(1)} %get-tuple-element.83), channel_id=1, source_target_pairs={{0,6},{1,7},{2,4},{3,5},{4,2},{5,3},{6,0},{7,1},{16,22},{17,23},{1... | collective-permute-start | bytes 516104 | tf_op jit(solution)/shard_map/ppermute | solution.py:308
  217.0 4.2 %collective-permute-done.36 = bf16[48,1792]{1,0:T(8,128)(2,1)S(1)} collective-permute-done((bf16[48,1792]{1,0:T(8,128)(2,1)S(1)}, bf16[48,1792]{1,0:T(8,128)(2,1)S(1)}, u32[]{:S(2)}, u32[]{:S(2)}) %collective-permute-start.36) | collective-permute-done | bytes 172064 | tf_op jit(solution)/shard_map/ppermute | solution.py:308
  222.8 3.4 collective-permute-start.38
  226.3 3.9 collective-permute-done.38
  242.4 99.5 %collective-permute-done.47.refs_1_ = bf16[48,1664]{1,0:T(8,128)(2,1)S(1)} collective-permute-done((bf16[48,1664]{1,0:T(8,128)(2,1)S(1)}, bf16[48,1664]{1,0:T(8,128)(2,1)S(1)}, u32[]{:S(2)}, u32[]{:S(2)}) %collective-permute-start.47) | collective-permute-done | bytes 159776 | tf_op jit(solution)/shard_map/ppermute | solution.py:324
  341.9 4.5 %collective-permute-done.48.refs_2_ = bf16[48,1664]{1,0:T(8,128)(2,1)S(1)} collective-permute-done((bf16[48,1664]{1,0:T(8,128)(2,1)S(1)}, bf16[48,1664]{1,0:T(8,128)(2,1)S(1)}, u32[]{:S(2)}, u32[]{:S(2)}) %collective-permute-start.48) | collective-permute-done | bytes 159776 | tf_op jit(solution)/shard_map/ppermute | solution.py:324
  346.5 3.7 collective-permute-done.50.refs_4_
  350.2 13.5 %shard_map.83 = (bf16[48,6656]{1,0:T(8,128)(2,1)S(1)}, bf16[48,1120]{1,0:T(8,128)(2,1)S(1)}, f32[1,6656]{1,0:T(1,128)S(1)}) custom-call(s32[2]{0:T(128)S(1)} %pad_add_fusion.1.refs_0_, bf16[48,1664]{1,0:T(8,128)(2,1)S(1)} %collective-permute-done.47.refs_1_, ...), custom_call_target="tpu_custom_call", output_to_operand_aliasing={{0}: (10, {}), {1}: (11, {}), {2}: (12, {})} | custom-call | flops 1431306240 | bytes 29818880 | tf_op jit(solution)/shard_map/pallas_call | solution.py:206
  369.6 12.6 %fusion = f32[1,6656,1120]{1,2,0:T(8,128)} fusion(bf16[48,1120]{1,0:T(8,128)(2,1)S(1)} %get-tuple-element.96, bf16[48,6656]{1,0:T(8,128)(2,1)S(1)} %get-tuple-element.72.refs_2_.refs_5_, f32[6656]{0:T(1024)S(1)} %reduce.1, f32[48]{0:T(128)S(1)} %slice_reduce_fusion), kind=kOutput, calls=%fused_computation.2 | convolution fusion | flops 724385792 | bytes 30592192 | tf_op jit(solution)/shard_map/dot_general | solution.py:47
  383.0 12.6 %fusion.1 = f32[1,6656,1120]{1,2,0:T(8,128)} fusion(bf16[48,6656]{1,0:T(8,128)(2,1)S(1)} %get-tuple-element.97, f32[48,1120]{1,0:T(8,128)S(1)} %get-tuple-element.74.refs_4_.refs_7_), kind=kOutput, calls=%fused_computation.3 | convolution fusion | flops 723591680 | bytes 30672896 | tf_op jit(solution)/shard_map/dot_general | solution.py:47
  (127 shorter events, 74.7 us)
Async XLA Ops:
  1.7 7.6 %collective-permute-start = (bf16[1,6,6656]{2,1,0:T(8,128)(2,1)S(1)}, bf16[1,6,6656]{2,1,0:T(8,128)(2,1)S(1)}, u32[]{:S(2)}, u32[]{:S(2)}) collective-permute-start(bf16[1,6,6656]{2,1,0:T(8,128)(2,1)S(1)} %broadcast_in_dim_reshape.3), channel_id=1, source_target_pairs={{0,1},{1,0},{2,3},{3,2},{4,5},{5,4},{6,7},{7,6},{24,25},{25,24},{2... | collective-permute-start | bytes 239624 | tf_op jit(solution)/shard_map/ppermute | solution.py:335
  9.3 7.8 %collective-permute-start.1 = (bf16[2,6,6656]{2,1,0:T(8,128)(2,1)S(1)}, bf16[2,6,6656]{2,1,0:T(8,128)(2,1)S(1)}, u32[]{:S(2)}, u32[]{:S(2)}) collective-permute-start(bf16[2,6,6656]{2,1,0:T(8,128)(2,1)S(1)} %pad_maximum_fusion.2), channel_id=1, source_target_pairs={{0,2},{1,3},{2,0},{3,1},{4,6},{5,7},{6,4},{7,5},{24,26},{25,27},{2... | collective-permute-start | bytes 479240 | tf_op jit(solution)/shard_map/ppermute | solution.py:335
  17.3 47.3 %collective-permute-start.2 = (bf16[4,6,6656]{2,1,0:T(8,128)(2,1)S(1)}, bf16[4,6,6656]{2,1,0:T(8,128)(2,1)S(1)}, u32[]{:S(2)}, u32[]{:S(2)}) collective-permute-start(bf16[4,6,6656]{2,1,0:T(8,128)(2,1)S(1)} %pad_maximum_fusion.1), channel_id=1, source_target_pairs={{0,4},{1,5},{2,6},{3,7},{4,0},{5,1},{6,2},{7,3},{24,28},{25,29},{2... | collective-permute-start | bytes 958472 | tf_op jit(solution)/shard_map/ppermute | solution.py:335
  78.4 10.1 %collective-permute-start.3 = (bf16[48,1664]{1,0:T(8,128)(2,1)S(1)}, bf16[48,1664]{1,0:T(8,128)(2,1)S(1)}, u32[]{:S(2)}, u32[]{:S(2)}) collective-permute-start(bf16[48,1664]{1,0:T(8,128)(2,1)S(1)} %get-tuple-element.52), channel_id=1, source_target_pairs={{0,6},{1,7},{2,4},{3,5},{4,2},{5,3},{6,0},{7,1},{16,22},{17,23},{1... | collective-permute-start | bytes 479240 | tf_op jit(solution)/shard_map/ppermute | solution.py:308
  81.7 10.2 %collective-permute-start.4 = (bf16[48,1664]{1,0:T(8,128)(2,1)S(1)}, bf16[48,1664]{1,0:T(8,128)(2,1)S(1)}, u32[]{:S(2)}, u32[]{:S(2)}) collective-permute-start(bf16[48,1664]{1,0:T(8,128)(2,1)S(1)} %get-tuple-element.53), channel_id=1, source_target_pairs={{0,4},{1,5},{2,6},{3,7},{4,0},{5,1},{6,2},{7,3},{16,20},{17,21},{1... | collective-permute-start | bytes 479240 | tf_op jit(solution)/shard_map/ppermute | solution.py:308
  85.3 8.2 %collective-permute-start.5 = (bf16[48,1664]{1,0:T(8,128)(2,1)S(1)}, bf16[48,1664]{1,0:T(8,128)(2,1)S(1)}, u32[]{:S(2)}, u32[]{:S(2)}) collective-permute-start(bf16[48,1664]{1,0:T(8,128)(2,1)S(1)} %get-tuple-element.54), channel_id=1, source_target_pairs={{0,2},{1,3},{2,0},{3,1},{4,6},{5,7},{6,4},{7,5},{16,18},{17,19},{1... | collective-permute-start | bytes 479240 | tf_op jit(solution)/shard_map/ppermute | solution.py:308
  93.5 7.2 %collective-permute-start.6 = (bf16[48,1664]{1,0:T(8,128)(2,1)S(1)}, bf16[48,1664]{1,0:T(8,128)(2,1)S(1)}, u32[]{:S(2)}, u32[]{:S(2)}) collective-permute-start(bf16[48,1664]{1,0:T(8,128)(2,1)S(1)} %add_convert_fusion.7), channel_id=1, source_target_pairs={{0,1},{1,0},{2,3},{3,2},{4,5},{5,4},{6,7},{7,6},{16,17},{17,16},{1... | collective-permute-start | bytes 479240 | tf_op jit(solution)/shard_map/ppermute | solution.py:315
  100.8 5.3 %collective-permute-start.10 = (bf16[48,1664]{1,0:T(8,128)(2,1)S(1)}, bf16[48,1664]{1,0:T(8,128)(2,1)S(1)}, u32[]{:S(2)}, u32[]{:S(2)}) collective-permute-start(bf16[48,1664]{1,0:T(8,128)(2,1)S(1)} %fusion.4), channel_id=1, source_target_pairs={{0,14},{1,15},{2,12},{3,13},{4,10},{5,11},{6,8},{7,9},{16,30},{17,... | collective-permute-start | bytes 479240 | tf_op jit(solution)/shard_map/ppermute | solution.py:324
  103.4 4.1 %collective-permute-start.8 = (bf16[48,1664]{1,0:T(8,128)(2,1)S(1)}, bf16[48,1664]{1,0:T(8,128)(2,1)S(1)}, u32[]{:S(2)}, u32[]{:S(2)}) collective-permute-start(bf16[48,1664]{1,0:T(8,128)(2,1)S(1)} %fusion.4), channel_id=1, source_target_pairs={{0,10},{1,11},{2,8},{3,9},{4,14},{5,15},{6,12},{7,13},{16,26},{17,... | collective-permute-start | bytes 479240 | tf_op jit(solution)/shard_map/ppermute | solution.py:324
  104.7 4.5 %collective-permute-start.9 = (bf16[48,1664]{1,0:T(8,128)(2,1)S(1)}, bf16[48,1664]{1,0:T(8,128)(2,1)S(1)}, u32[]{:S(2)}, u32[]{:S(2)}) collective-permute-start(bf16[48,1664]{1,0:T(8,128)(2,1)S(1)} %fusion.4), channel_id=1, source_target_pairs={{0,12},{1,13},{2,14},{3,15},{4,8},{5,9},{6,10},{7,11},{16,28},{17,... | collective-permute-start | bytes 479240 | tf_op jit(solution)/shard_map/ppermute | solution.py:324
  117.1 10.1 %collective-permute-start.19 = (bf16[48,1664]{1,0:T(8,128)(2,1)S(1)}, bf16[48,1664]{1,0:T(8,128)(2,1)S(1)}, u32[]{:S(2)}, u32[]{:S(2)}) collective-permute-start(bf16[48,1664]{1,0:T(8,128)(2,1)S(1)} %get-tuple-element.66), channel_id=1, source_target_pairs={{0,6},{1,7},{2,4},{3,5},{4,2},{5,3},{6,0},{7,1},{16,22},{17,23},{1... | collective-permute-start | bytes 479240 | tf_op jit(solution)/shard_map/ppermute | solution.py:308
  120.4 10.3 %collective-permute-start.20 = (bf16[48,1664]{1,0:T(8,128)(2,1)S(1)}, bf16[48,1664]{1,0:T(8,128)(2,1)S(1)}, u32[]{:S(2)}, u32[]{:S(2)}) collective-permute-start(bf16[48,1664]{1,0:T(8,128)(2,1)S(1)} %get-tuple-element.67), channel_id=1, source_target_pairs={{0,4},{1,5},{2,6},{3,7},{4,0},{5,1},{6,2},{7,3},{16,20},{17,21},{1... | collective-permute-start | bytes 479240 | tf_op jit(solution)/shard_map/ppermute | solution.py:308
  122.9 9.4 %collective-permute-start.21 = (bf16[48,1664]{1,0:T(8,128)(2,1)S(1)}, bf16[48,1664]{1,0:T(8,128)(2,1)S(1)}, u32[]{:S(2)}, u32[]{:S(2)}) collective-permute-start(bf16[48,1664]{1,0:T(8,128)(2,1)S(1)} %get-tuple-element.68), channel_id=1, source_target_pairs={{0,2},{1,3},{2,0},{3,1},{4,6},{5,7},{6,4},{7,5},{16,18},{17,19},{1... | collective-permute-start | bytes 479240 | tf_op jit(solution)/shard_map/ppermute | solution.py:308
  132.4 7.2 %collective-permute-start.22 = (bf16[48,1664]{1,0:T(8,128)(2,1)S(1)}, bf16[48,1664]{1,0:T(8,128)(2,1)S(1)}, u32[]{:S(2)}, u32[]{:S(2)}) collective-permute-start(bf16[48,1664]{1,0:T(8,128)(2,1)S(1)} %add_convert_fusion.4), channel_id=1, source_target_pairs={{0,1},{1,0},{2,3},{3,2},{4,5},{5,4},{6,7},{7,6},{16,17},{17,16},{1... | collective-permute-start | bytes 479240 | tf_op jit(solution)/shard_map/ppermute | solution.py:315
  139.6 27.2 %collective-permute-start.23 = (bf16[48,1664]{1,0:T(8,128)(2,1)S(1)}, bf16[48,1664]{1,0:T(8,128)(2,1)S(1)}, u32[]{:S(2)}, u32[]{:S(2)}) collective-permute-start(bf16[48,1664]{1,0:T(8,128)(2,1)S(1)} %add_convert_fusion.3), channel_id=1, source_target_pairs={{0,8},{1,9},{2,10},{3,11},{4,12},{5,13},{6,14},{7,15},{16,24},{17,... | collective-permute-start | bytes 479240 | tf_op jit(solution)/shard_map/ppermute | solution.py:324
  159.0 7.8 %collective-permute-start.24 = (bf16[48,1664]{1,0:T(8,128)(2,1)S(1)}, bf16[48,1664]{1,0:T(8,128)(2,1)S(1)}, u32[]{:S(2)}, u32[]{:S(2)}) collective-permute-start(bf16[48,1664]{1,0:T(8,128)(2,1)S(1)} %add_convert_fusion.3), channel_id=1, source_target_pairs={{0,10},{1,11},{2,8},{3,9},{4,14},{5,15},{6,12},{7,13},{16,26},{17,... | collective-permute-start | bytes 479240 | tf_op jit(solution)/shard_map/ppermute | solution.py:324
  163.1 5.0 %collective-permute-start.25 = (bf16[48,1664]{1,0:T(8,128)(2,1)S(1)}, bf16[48,1664]{1,0:T(8,128)(2,1)S(1)}, u32[]{:S(2)}, u32[]{:S(2)}) collective-permute-start(bf16[48,1664]{1,0:T(8,128)(2,1)S(1)} %add_convert_fusion.3), channel_id=1, source_target_pairs={{0,12},{1,13},{2,14},{3,15},{4,8},{5,9},{6,10},{7,11},{16,28},{17,... | collective-permute-start | bytes 479240 | tf_op jit(solution)/shard_map/ppermute | solution.py:324
  165.4 4.5 %collective-permute-start.26 = (bf16[48,1664]{1,0:T(8,128)(2,1)S(1)}, bf16[48,1664]{1,0:T(8,128)(2,1)S(1)}, u32[]{:S(2)}, u32[]{:S(2)}) collective-permute-start(bf16[48,1664]{1,0:T(8,128)(2,1)S(1)} %add_convert_fusion.3), channel_id=1, source_target_pairs={{0,14},{1,15},{2,12},{3,13},{4,10},{5,11},{6,8},{7,9},{16,30},{17,... | collective-permute-start | bytes 479240 | tf_op jit(solution)/shard_map/ppermute | solution.py:324
  175.0 22.8 %collective-permute-start.31 = (bf16[48,1664]{1,0:T(8,128)(2,1)S(1)}, bf16[48,1664]{1,0:T(8,128)(2,1)S(1)}, u32[]{:S(2)}, u32[]{:S(2)}) collective-permute-start(bf16[48,1664]{1,0:T(8,128)(2,1)S(1)} %fusion.5), channel_id=1, source_target_pairs={{8,0},{9,1},{10,2},{11,3},{12,4},{13,5},{14,6},{15,7},{24,16},{25,... | collective-permute-start | bytes 479240 | tf_op jit(solution)/shard_map/ppermute | solution.py:324
  176.3 26.0 %collective-permute-start.32 = (bf16[48,1664]{1,0:T(8,128)(2,1)S(1)}, bf16[48,1664]{1,0:T(8,128)(2,1)S(1)}, u32[]{:S(2)}, u32[]{:S(2)}) collective-permute-start(bf16[48,1664]{1,0:T(8,128)(2,1)S(1)} %fusion.5), channel_id=1, source_target_pairs={{8,2},{9,3},{10,0},{11,1},{12,6},{13,7},{14,4},{15,5},{24,18},{25,... | collective-permute-start | bytes 479240 | tf_op jit(solution)/shard_map/ppermute | solution.py:324
  177.6 24.7 %collective-permute-start.33 = (bf16[48,1664]{1,0:T(8,128)(2,1)S(1)}, bf16[48,1664]{1,0:T(8,128)(2,1)S(1)}, u32[]{:S(2)}, u32[]{:S(2)}) collective-permute-start(bf16[48,1664]{1,0:T(8,128)(2,1)S(1)} %fusion.5), channel_id=1, source_target_pairs={{8,4},{9,5},{10,6},{11,7},{12,0},{13,1},{14,2},{15,3},{24,20},{25,... | collective-permute-start | bytes 479240 | tf_op jit(solution)/shard_map/ppermute | solution.py:324
  178.9 26.9 %collective-permute-start.34 = (bf16[48,1664]{1,0:T(8,128)(2,1)S(1)}, bf16[48,1664]{1,0:T(8,128)(2,1)S(1)}, u32[]{:S(2)}, u32[]{:S(2)}) collective-permute-start(bf16[48,1664]{1,0:T(8,128)(2,1)S(1)} %fusion.5), channel_id=1, source_target_pairs={{8,6},{9,7},{10,4},{11,5},{12,2},{13,3},{14,0},{15,1},{24,22},{25,... | collective-permute-start | bytes 479240 | tf_op jit(solution)/shard_map/ppermute | solution.py:324
  206.9 10.1 %collective-permute-start.35 = (bf16[48,1792]{1,0:T(8,128)(2,1)S(1)}, bf16[48,1792]{1,0:T(8,128)(2,1)S(1)}, u32[]{:S(2)}, u32[]{:S(2)}) collective-permute-start(bf16[48,1792]{1,0:T(8,128)(2,1)S(1)} %get-tuple-element.83), channel_id=1, source_target_pairs={{0,6},{1,7},{2,4},{3,5},{4,2},{5,3},{6,0},{7,1},{16,22},{17,23},{1... | collective-permute-start | bytes 516104 | tf_op jit(solution)/shard_map/ppermute | solution.py:308
  211.1 10.2 %collective-permute-start.36 = (bf16[48,1792]{1,0:T(8,128)(2,1)S(1)}, bf16[48,1792]{1,0:T(8,128)(2,1)S(1)}, u32[]{:S(2)}, u32[]{:S(2)}) collective-permute-start(bf16[48,1792]{1,0:T(8,128)(2,1)S(1)} %get-tuple-element.84), channel_id=1, source_target_pairs={{0,4},{1,5},{2,6},{3,7},{4,0},{5,1},{6,2},{7,3},{16,20},{17,21},{1... | collective-permute-start | bytes 516104 | tf_op jit(solution)/shard_map/ppermute | solution.py:308
  214.1 8.7 %collective-permute-start.37 = (bf16[48,1792]{1,0:T(8,128)(2,1)S(1)}, bf16[48,1792]{1,0:T(8,128)(2,1)S(1)}, u32[]{:S(2)}, u32[]{:S(2)}) collective-permute-start(bf16[48,1792]{1,0:T(8,128)(2,1)S(1)} %get-tuple-element.85), channel_id=1, source_target_pairs={{0,2},{1,3},{2,0},{3,1},{4,6},{5,7},{6,4},{7,5},{16,18},{17,19},{1... | collective-permute-start | bytes 516104 | tf_op jit(solution)/shard_map/ppermute | solution.py:308
  222.8 7.3 %collective-permute-start.38 = (bf16[48,1792]{1,0:T(8,128)(2,1)S(1)}, bf16[48,1792]{1,0:T(8,128)(2,1)S(1)}, u32[]{:S(2)}, u32[]{:S(2)}) collective-permute-start(bf16[48,1792]{1,0:T(8,128)(2,1)S(1)} %add_convert_fusion.1), channel_id=1, source_target_pairs={{0,1},{1,0},{2,3},{3,2},{4,5},{5,4},{6,7},{7,6},{16,17},{17,16},{1... | collective-permute-start | bytes 516104 | tf_op jit(solution)/shard_map/ppermute | solution.py:315
  237.2 104.7 %collective-permute-start.47 = (bf16[48,1664]{1,0:T(8,128)(2,1)S(1)}, bf16[48,1664]{1,0:T(8,128)(2,1)S(1)}, u32[]{:S(2)}, u32[]{:S(2)}) collective-permute-start(bf16[48,1664]{1,0:T(8,128)(2,1)S(1)} %fusion.9), channel_id=1, source_target_pairs={{8,0},{9,1},{10,2},{11,3},{12,4},{13,5},{14,6},{15,7},{24,16},{25,... | collective-permute-start | bytes 479240 | tf_op jit(solution)/shard_map/ppermute | solution.py:324
  238.5 108.0 %collective-permute-start.48 = (bf16[48,1664]{1,0:T(8,128)(2,1)S(1)}, bf16[48,1664]{1,0:T(8,128)(2,1)S(1)}, u32[]{:S(2)}, u32[]{:S(2)}) collective-permute-start(bf16[48,1664]{1,0:T(8,128)(2,1)S(1)} %fusion.9), channel_id=1, source_target_pairs={{8,2},{9,3},{10,0},{11,1},{12,6},{13,7},{14,4},{15,5},{24,18},{25,... | collective-permute-start | bytes 479240 | tf_op jit(solution)/shard_map/ppermute | solution.py:324
  239.8 106.7 %collective-permute-start.49 = (bf16[48,1664]{1,0:T(8,128)(2,1)S(1)}, bf16[48,1664]{1,0:T(8,128)(2,1)S(1)}, u32[]{:S(2)}, u32[]{:S(2)}) collective-permute-start(bf16[48,1664]{1,0:T(8,128)(2,1)S(1)} %fusion.9), channel_id=1, source_target_pairs={{8,4},{9,5},{10,6},{11,7},{12,0},{13,1},{14,2},{15,3},{24,20},{25,... | collective-permute-start | bytes 479240 | tf_op jit(solution)/shard_map/ppermute | solution.py:324
  241.1 109.1 %collective-permute-start.50 = (bf16[48,1664]{1,0:T(8,128)(2,1)S(1)}, bf16[48,1664]{1,0:T(8,128)(2,1)S(1)}, u32[]{:S(2)}, u32[]{:S(2)}) collective-permute-start(bf16[48,1664]{1,0:T(8,128)(2,1)S(1)} %fusion.9), channel_id=1, source_target_pairs={{8,6},{9,7},{10,4},{11,5},{12,2},{13,3},{14,0},{15,1},{24,22},{25,... | collective-permute-start | bytes 479240 | tf_op jit(solution)/shard_map/ppermute | solution.py:324
  367.6 14.6 %collective-permute-start.52 = (f32[1,6656]{1,0:T(1,128)S(1)}, f32[1,6656]{1,0:T(1,128)S(1)}, u32[]{:S(2)}, u32[]{:S(2)}) collective-permute-start(f32[1,6656]{1,0:T(1,128)S(1)} %add.164), channel_id=1, source_target_pairs={{0,2},{1,3},{2,0},{3,1},{4,6},{5,7},{6,4},{7,5},{8,10},{9,11},{10,... | collective-permute-start | bytes 79880 | tf_op jit(solution)/shard_map/ppermute | solution.py:345
  382.2 13.4 %collective-permute-start.53 = (f32[1,6656]{1,0:T(1,128)S(1)}, f32[1,6656]{1,0:T(1,128)S(1)}, u32[]{:S(2)}, u32[]{:S(2)}) collective-permute-start(f32[1,6656]{1,0:T(1,128)S(1)} %add.165), channel_id=1, source_target_pairs={{0,4},{1,5},{2,6},{3,7},{4,0},{5,1},{6,2},{7,3},{8,12},{9,13},{10,... | collective-permute-start | bytes 79880 | tf_op jit(solution)/shard_map/ppermute | solution.py:345
  (23 other events, 58.2 us)

commit v3 on v1

v3 whole, which is shorter than its diff:
```python
import functools
import math

import jax
import jax.numpy as jnp
from jax import lax
from jax.experimental import pallas as pl
from jax.experimental.pallas import tpu as pltpu
from jax.sharding import PartitionSpec as P

D = 6656
HIDDEN_SIZE = 8960


EPSILON = 1e-05
GELU_SCALE = 0.7978845608028654
GELU_CUBIC = 0.044715

INV_WIDTH = 1.0 / math.sqrt(D)
INV_HIDDEN = 1.0 / math.sqrt(HIDDEN_SIZE)

AXES = ("section", "dp")
QUARTERS = 4
LANES = 128
BLOCK = 128
SLOTS = 3
STAGE_BYTES = 32 * 1024 * 1024
FINAL_BYTES = 52 * 1024 * 1024

ANY = pl.BlockSpec(memory_space=pl.ANY)
VMEM = pl.BlockSpec(memory_space=pltpu.VMEM)
SMEM = pl.BlockSpec(memory_space=pltpu.SMEM)


def gelu_value(preact):
    inner = GELU_SCALE * (preact + GELU_CUBIC * preact * preact * preact)
    return 0.5 * preact * (1.0 + jnp.tanh(inner))


def gelu_slope(preact):
    inner = GELU_SCALE * (preact + GELU_CUBIC * preact * preact * preact)
    tangent = jnp.tanh(inner)
    return 0.5 * (1.0 + tangent) + 0.5 * preact * (1.0 - tangent * tangent) * GELU_SCALE * (
        1.0 + 3.0 * GELU_CUBIC * preact * preact
    )


def outer_rows(left, right):
    return lax.dot_general(
        left, right, (((0,), (0,)), ((), ())), preferred_element_type=jnp.float32
    )


def across_hidden(left, right):
    return lax.dot_general(
        left, right, (((1,), (1,)), ((), ())), preferred_element_type=jnp.float32
    )


def plain_product(left, right):
    return jnp.dot(left, right, preferred_element_type=jnp.float32)


FAR, NEAR = (3, 2), (1, 0)


def quarter(place_ref, k, width):
    start = (place_ref[1] ^ k) * width
    return pl.ds(pl.multiple_of(start, LANES), width)


def read_quarter(place_ref, piece_refs, k, width):
    if len(piece_refs) == 1:
        return piece_refs[0][:, quarter(place_ref, k, width)]
    return piece_refs[k][...]


def write_out(copies):
    for copy in copies:
        copy.start()
    for copy in copies:
        copy.wait()


def quarter_copies(place_ref, piece_refs, target, sems, width):
    if len(piece_refs) == 1:
        return [pltpu.make_async_copy(piece_refs[0], target, sems.at[0])]
    return [
        pltpu.make_async_copy(ref, target.at[:, quarter(place_ref, k, width)], sems.at[k])
        for k, ref in enumerate(piece_refs)
    ]


def weight_copies(place_ref, source, buffer_ref, sems, quarters):
    width = buffer_ref.shape[2]
    return [
        pltpu.make_async_copy(
            source.at[:, quarter(place_ref, k, width)], buffer_ref.at[at], sems.at[at]
        )
        for at, k in enumerate(quarters)
    ]


def contract_width(buffer_ref, copies, read):
    total = None
    for k in range(QUARTERS):
        copies[k].wait()
        part = across_hidden(read(k), buffer_ref[k])
        total = part if total is None else total + part
    return total


def enter_section(place_ref, piece_refs, gain_ref, up_ref, up_copies, width):
    squares = 0.0
    for k in range(QUARTERS):
        values = read_quarter(place_ref, piece_refs, k, width).astype(jnp.float32)
        squares = squares + jnp.sum(values * values, axis=-1, keepdims=True)
    norm_scale = lax.rsqrt(squares * (1.0 / (QUARTERS * width)) + EPSILON)

    def read(k):
        normed = read_quarter(place_ref, piece_refs, k, width).astype(jnp.float32) * norm_scale
        return (normed * gain_ref[:, quarter(place_ref, k, width)]).astype(jnp.bfloat16)

    return (norm_scale, contract_width(up_ref, up_copies, read) * INV_WIDTH)


def hidden_part(part_refs, hidden, down_ref, copies):
    for at, ref in enumerate(part_refs):
        copies[at].wait()
        ref[...] = (plain_product(hidden, down_ref[at]) * INV_HIDDEN).astype(jnp.bfloat16)


def scaled_part(part_refs, quarters, preact_grad, along, rows_of, up_ref, copies, gain_ref):
    width = up_ref.shape[2]
    for at, k in enumerate(quarters):
        if copies:
            copies[at].wait()
        part = plain_product(preact_grad, up_ref[at if copies else k]) * INV_WIDTH
        gain_ref[at] = jnp.sum(part * rows_of(k), axis=0, keepdims=True)
        part_refs[at][:, :width] = part.astype(jnp.bfloat16)
        part_refs[at][:, width:] = along


def along_rows(preact_grad, preact):
    total = jnp.sum(preact_grad.astype(jnp.float32) * preact, axis=-1, keepdims=True)
    return jnp.broadcast_to(total.astype(jnp.bfloat16), (total.shape[0], LANES))


def gain_copies(place_ref, gain_ref, target, quarters, sems):
    return [
        pltpu.make_async_copy(gain_ref.at[at], target.at[place_ref[1] ^ k], sems.at[at])
        for at, k in enumerate(quarters)
    ]


def forward_far(section, pieces, with_stash, place_ref, *refs):
    piece_refs, refs = refs[:pieces], refs[pieces:]
    gain_ref, up_hbm, down_hbm = refs[:3]
    refs = refs[3 + (4 if with_stash else 0) :]
    part_refs, hidden_ref = refs[:2], refs[2]
    rows_out, scale_out, preact_out, own_out, scale_ref, preact_ref, own_ref, sems = refs[3:11]
    up_ref, down_ref, up_sems, down_sems = refs[11:]
    width = up_ref.shape[2]

    @pl.when(place_ref[0] == section)
    def _():
        up_copies = weight_copies(place_ref, up_hbm, up_ref, up_sems, range(QUARTERS))
        down_copies = weight_copies(place_ref, down_hbm, down_ref, down_sems, FAR)
        copies = quarter_copies(place_ref, piece_refs, rows_out, sems, width)
        for copy in up_copies + down_copies + copies:
            copy.start()
        norm_scale, preact = enter_section(
            place_ref, piece_refs, gain_ref, up_ref, up_copies, width
        )
        scale_ref[...] = jnp.broadcast_to(norm_scale, scale_ref.shape)
        preact_ref[...] = preact
        own_rows = read_quarter(place_ref, piece_refs, 0, width)
        own_ref[...] = own_rows.astype(jnp.float32) * norm_scale
        more = [
            pltpu.make_async_copy(scale_ref, scale_out, sems.at[QUARTERS]),
            pltpu.make_async_copy(preact_ref, preact_out, sems.at[QUARTERS + 1]),
            pltpu.make_async_copy(own_ref, own_out, sems.at[QUARTERS + 2]),
        ]
        for copy in more:
            copy.start()
        hidden = gelu_value(preact).astype(jnp.bfloat16)
        hidden_ref[...] = hidden
        hidden_part(part_refs, hidden, down_ref, down_copies)
        for copy in copies + more:
            copy.wait()


def forward_near(section, place_ref, hidden_ref, down_hbm, first_ref, second_ref, down_ref, sems):
    @pl.when(place_ref[0] == section)
    def _():
        copies = weight_copies(place_ref, down_hbm, down_ref, sems, NEAR)
        for copy in copies:
            copy.start()
        hidden_part([first_ref, second_ref], hidden_ref[...], down_ref, copies)


def early_grad(
    section, place_ref, rows_ref, down_hbm, grad_out, hidden_grad_out,
    total_ref, sems, down_ref, down_sems,
):
    width = down_ref.shape[2]

    @pl.when(place_ref[0] == section)
    def _():
        first = pltpu.make_async_copy(rows_ref, grad_out, sems.at[0])
        down_copies = weight_copies(place_ref, down_hbm, down_ref, down_sems, range(QUARTERS))
        for copy in down_copies + [first]:
            copy.start()
        total_ref[...] = INV_HIDDEN * contract_width(
            down_ref, down_copies, lambda k: read_quarter(place_ref, [rows_ref], k, width)
        )
        second = pltpu.make_async_copy(total_ref, hidden_grad_out, sems.at[1])
        second.start()
        first.wait()
        second.wait()


def last_far(section, place_ref, *refs):
    piece_refs, refs = refs[:QUARTERS], refs[QUARTERS:]
    hidden_grad_ref, gain_row_ref, up_hbm = refs[:3]
    refs = refs[7:]
    part_refs, preact_grad_ref, along_ref = refs[:2], refs[2], refs[3]
    rows_out, scale_out, preact_out, own_out, preact_grad_out, gain_out = refs[4:10]
    scale_ref, preact_ref, own_ref, gain_ref, sems, up_ref, up_sems = refs[10:]
    width = up_ref.shape[2]

    @pl.when(place_ref[0] == section)
    def _():
        up_copies = weight_copies(place_ref, up_hbm, up_ref, up_sems, range(QUARTERS))
        copies = quarter_copies(place_ref, piece_refs, rows_out, sems, width)
        for copy in up_copies + copies:
            copy.start()
        norm_scale, preact = enter_section(
            place_ref, piece_refs, gain_row_ref, up_ref, up_copies, width
        )
        preact_grad = (hidden_grad_ref[...] * gelu_slope(preact)).astype(jnp.bfloat16)
        along = along_rows(preact_grad, preact)
        scale_ref[...] = jnp.broadcast_to(norm_scale, scale_ref.shape)
        preact_ref[...] = preact
        preact_grad_ref[...] = preact_grad
        along_ref[...] = along
        own_ref[...] = piece_refs[0][...].astype(jnp.float32) * norm_scale
        more = [
            pltpu.make_async_copy(scale_ref, scale_out, sems.at[QUARTERS]),
            pltpu.make_async_copy(preact_ref, preact_out, sems.at[QUARTERS + 1]),
            pltpu.make_async_copy(own_ref, own_out, sems.at[QUARTERS + 2]),
            pltpu.make_async_copy(preact_grad_ref, preact_grad_out, sems.at[QUARTERS + 3]),
        ]
        for copy in more:
            copy.start()

        def rows_of(k):
            return piece_refs[k][...].astype(jnp.float32) * norm_scale

        scaled_part(part_refs, FAR, preact_grad, along, rows_of, up_ref, [], gain_ref)
        write_out(gain_copies(place_ref, gain_ref, gain_out, FAR, sems.at[pl.ds(QUARTERS + 4, 2)]))
        for copy in copies + more:
            copy.wait()


def backward_far(section, place_ref, *refs):
    piece_refs, refs = refs[:QUARTERS], refs[QUARTERS:]
    rows_ref, scale_ref, preact_ref, up_hbm, down_hbm = refs[:5]
    refs = refs[8:]
    part_refs, preact_grad_ref, along_ref = refs[:2], refs[2], refs[3]
    grad_out, preact_grad_out, gain_out, gain_ref, sems = refs[4:9]
    up_ref, down_ref, up_sems, down_sems = refs[9:]
    width = up_ref.shape[2]

    @pl.when(place_ref[0] == section)
    def _():
        down_copies = weight_copies(place_ref, down_hbm, down_ref, down_sems, range(QUARTERS))
        up_copies = weight_copies(place_ref, up_hbm, up_ref, up_sems, FAR)
        copies = quarter_copies(place_ref, piece_refs, grad_out, sems, width)
        for copy in down_copies + up_copies + copies:
            copy.start()
        hidden_grad = INV_HIDDEN * contract_width(
            down_ref, down_copies, lambda k: piece_refs[k][...]
        )
        preact = preact_ref[...]
        preact_grad = (hidden_grad * gelu_slope(preact)).astype(jnp.bfloat16)
        along = along_rows(preact_grad, preact)
        preact_grad_ref[...] = preact_grad
        along_ref[...] = along
        more = pltpu.make_async_copy(preact_grad_ref, preact_grad_out, sems.at[QUARTERS])
        more.start()
        norm_scale = scale_ref[:, :1]

        def rows_of(k):
            return rows_ref[:, quarter(place_ref, k, width)].astype(jnp.float32) * norm_scale

        scaled_part(
            part_refs, FAR, preact_grad, along, rows_of, up_ref, up_copies, gain_ref
        )
        write_out(gain_copies(place_ref, gain_ref, gain_out, FAR, sems.at[pl.ds(QUARTERS + 1, 2)]))
        for copy in copies + [more]:
            copy.wait()


def backward_near(
    section, place_ref, preact_grad_ref, along_ref, rows_ref, scale_ref, up_hbm, gain_in,
    first_ref, second_ref, gain_out, gain_ref, sems, up_ref, up_sems,
):
    del gain_in
    width = up_ref.shape[2]

    @pl.when(place_ref[0] == section)
    def _():
        copies = weight_copies(place_ref, up_hbm, up_ref, up_sems, NEAR)
        for copy in copies:
            copy.start()
        norm_scale = scale_ref[:, :1]

        def rows_of(k):
            return rows_ref[:, quarter(place_ref, k, width)].astype(jnp.float32) * norm_scale

        scaled_part(
            [first_ref, second_ref], NEAR, preact_grad_ref[...], along_ref[...],
            rows_of, up_ref, copies, gain_ref,
        )
        write_out(gain_copies(place_ref, gain_ref, gain_out, NEAR, sems))


def hidden_blocks(local):
    return [(start, min(BLOCK, local - start)) for start in range(0, local, BLOCK)]


def outer_blocks(left_ref, right_ref, factor, blocks, target, buffer_ref, sems, beside):
    copies = []
    for i, (start, size) in enumerate(blocks):
        slot = i % SLOTS
        if i >= SLOTS:
            copies[i - SLOTS].wait()
        value = outer_rows(left_ref[:, start : start + size], right_ref[...])
        buffer_ref[slot, :size] = value * factor
        copy = pltpu.make_async_copy(
            buffer_ref.at[slot, pl.ds(0, size)], target.at[pl.ds(start, size)], sems.at[slot]
        )
        copy.start()
        copies.append(copy)
        if i < len(beside):
            beside[i]()
    for run in beside[len(blocks) :]:
        run()
    for copy in copies[-SLOTS:]:
        copy.wait()


def final_down(section, place_ref, *refs):
    piece_refs, refs = refs[:QUARTERS], refs[QUARTERS:]
    grad_in, preact_grad_in, gain_in, rows_ref, scale_ref, preact_ref, gain_row_ref = refs[:7]
    up_hbm, down_hbm = refs[7:9]
    target, preact_grad_ref, gain_ref, scaled_ref = refs[9:13]
    grad_ref, hidden_ref, hidden_grad_ref, buffer_ref, sems = refs[13:18]
    up_ref, down_ref, up_sems, down_sems = refs[18:]
    width = up_ref.shape[2]
    active = place_ref[0] == section
    down_copies = weight_copies(place_ref, down_hbm, down_ref, down_sems, range(QUARTERS))
    up_copies = weight_copies(place_ref, up_hbm, up_ref, up_sems, range(QUARTERS))

    @pl.when(active)
    def _():
        for copy in down_copies + up_copies:
            copy.start()
        for k in range(QUARTERS):
            grad_ref[:, quarter(place_ref, k, width)] = piece_refs[k][...]

    @pl.when(jnp.logical_not(active))
    def _():
        grad_ref[...] = grad_in[...]
        preact_grad_ref[...] = preact_grad_in[...]
        gain_ref[...] = gain_in[...]

    norm_scale = scale_ref[:, :1]
    hidden_ref[...] = gelu_value(preact_ref[...]).astype(jnp.bfloat16)

    def add_grad(k):
        @pl.when(active)
        def _():
            down_copies[k].wait()
            part = across_hidden(piece_refs[k][...], down_ref[k])
            hidden_grad_ref[...] = part if k == 0 else hidden_grad_ref[...] + part

    def finish_grad():
        @pl.when(active)
        def _():
            hidden_grad = hidden_grad_ref[...] * INV_HIDDEN
            preact_grad_ref[...] = (hidden_grad * gelu_slope(preact_ref[...])).astype(jnp.bfloat16)

    def add_gain(k):
        @pl.when(active)
        def _():
            up_copies[k].wait()
            part = plain_product(preact_grad_ref[...], up_ref[k]) * INV_WIDTH
            rows = rows_ref[:, quarter(place_ref, k, width)]
            normed = rows.astype(jnp.float32) * norm_scale
            gain_ref[place_ref[1] ^ k] = jnp.sum(part * normed, axis=0, keepdims=True)

    def scale_rows():
        normed = rows_ref[...].astype(jnp.float32) * norm_scale
        scaled_ref[...] = (normed * gain_row_ref[...]).astype(jnp.bfloat16)

    beside = [functools.partial(add_grad, k) for k in range(QUARTERS)]
    beside += [finish_grad] + [functools.partial(add_gain, k) for k in range(QUARTERS)]
    beside += [scale_rows]
    blocks = hidden_blocks(target.shape[0])
    outer_blocks(hidden_ref, grad_ref, INV_HIDDEN, blocks, target, buffer_ref, sems, beside)


def final_up(blocks, preact_grad_ref, scaled_ref, *refs):
    target, buffer_ref, sems = refs[-3:]
    outer_blocks(preact_grad_ref, scaled_ref, INV_WIDTH, blocks, target, buffer_ref, sems, [])


def struct(*shape, dtype=jnp.bfloat16):
    return jax.ShapeDtypeStruct(shape, dtype)


def call(kernel, inputs, specs, outputs, out_specs, scratch, aliases, limit, products):
    flops = sum(2 * a * b * c for a, b, c in products)
    return pl.pallas_call(
        kernel,
        out_shape=outputs,
        in_specs=specs,
        out_specs=out_specs,
        scratch_shapes=scratch,
        input_output_aliases=aliases,
        cost_estimate=pl.CostEstimate(
            flops=flops,
            bytes_accessed=sum(2 * b * c for _, b, c in products),
            transcendentals=0,
        ),
        compiler_params=pltpu.CompilerParams(vmem_limit_bytes=limit),
    )(*inputs)


def lay_rows(place_ref, held_ref, gain_ref, rows_ref, own_ref, own_gain_ref):
    count, micro, tokens, width = held_ref.shape
    for i in range(count):
        for j in range(micro):
            start = (i * micro + j) * tokens
            rows_ref[start : start + tokens, :] = held_ref[i, j]
    own = quarter(place_ref, 0, width // QUARTERS)
    own_ref[...] = rows_ref[:, own]
    own_gain_ref[...] = gain_ref[:, own]


def run_lay_rows(place, held, gain):
    rows, width = held.size // held.shape[-1], held.shape[-1]
    return call(
        lay_rows,
        [place, held, gain],
        [SMEM, VMEM, VMEM],
        [
            struct(rows, width),
            struct(rows, width // QUARTERS),
            struct(1, width // QUARTERS, dtype=jnp.float32),
        ],
        [VMEM] * 3,
        [],
        {},
        STAGE_BYTES,
        [],
    )


def weight_buffer(up, quarters):
    return pltpu.VMEM((quarters, up.shape[0], up.shape[1] // QUARTERS), up.dtype)


def weight_sems(quarters):
    return pltpu.SemaphoreType.DMA((quarters,))


def run_forward_far(section, place, pieces, gain, up, down, stash):
    rows, (local, width) = pieces[0].shape[0], up.shape
    part = struct(rows, width // QUARTERS)
    first = 4 + len(pieces)
    result = call(
        functools.partial(forward_far, section, len(pieces), bool(stash)),
        [place, *pieces, gain, up, down, *stash],
        [SMEM] + [VMEM] * (len(pieces) + 1) + [ANY] * (2 + len(stash)),
        [
            part,
            part,
            struct(rows, local),
            struct(rows, width),
            struct(rows, LANES, dtype=jnp.float32),
            struct(rows, local, dtype=jnp.float32),
            struct(rows, width // QUARTERS, dtype=jnp.float32),
        ],
        [VMEM] * 3 + [ANY] * 4,
        [
            pltpu.VMEM((rows, LANES), jnp.float32),
            pltpu.VMEM((rows, local), jnp.float32),
            pltpu.VMEM((rows, width // QUARTERS), jnp.float32),
            pltpu.SemaphoreType.DMA((QUARTERS + 3,)),
            weight_buffer(up, QUARTERS),
            weight_buffer(up, 2),
            weight_sems(QUARTERS),
            weight_sems(2),
        ],
        {first + i: 3 + i for i in range(len(stash))},
        STAGE_BYTES,
        [(rows, width, local), (rows, local, width // 2)],
    )
    return (result[:2], result[2], result[3:])


def run_forward_near(section, place, hidden, down):
    rows, (local, width) = hidden.shape[0], down.shape
    part = struct(rows, width // QUARTERS)
    return call(
        functools.partial(forward_near, section),
        [place, hidden, down],
        [SMEM, VMEM, ANY],
        [part, part],
        [VMEM] * 2,
        [weight_buffer(down, 2), weight_sems(2)],
        {},
        STAGE_BYTES,
        [(rows, local, width // 2)],
    )


def run_early_grad(section, place, entered, down):
    rows, (local, width) = entered.shape[0], down.shape
    return call(
        functools.partial(early_grad, section),
        [place, entered, down],
        [SMEM, VMEM, ANY],
        [struct(rows, width), struct(rows, local, dtype=jnp.float32)],
        [ANY] * 2,
        [
            pltpu.VMEM((rows, local), jnp.float32),
            pltpu.SemaphoreType.DMA((2,)),
            weight_buffer(down, QUARTERS),
            weight_sems(QUARTERS),
        ],
        {},
        STAGE_BYTES,
        [(rows, width, local)],
    )


def run_last_far(section, place, pieces, hidden_grad, gain, up, stash):
    rows, (local, width) = pieces[0].shape[0], up.shape
    part = struct(rows, width // QUARTERS + LANES)
    result = call(
        functools.partial(last_far, section),
        [place, *pieces, hidden_grad, gain, up, *stash],
        [SMEM] + [VMEM] * (QUARTERS + 2) + [ANY] * 5,
        [
            part,
            part,
            struct(rows, local),
            struct(rows, LANES),
            struct(rows, width),
            struct(rows, LANES, dtype=jnp.float32),
            struct(rows, local, dtype=jnp.float32),
            struct(rows, width // QUARTERS, dtype=jnp.float32),
            struct(rows, local),
            struct(QUARTERS, 1, width // QUARTERS, dtype=jnp.float32),
        ],
        [VMEM] * 4 + [ANY] * 6,
        [
            pltpu.VMEM((rows, LANES), jnp.float32),
            pltpu.VMEM((rows, local), jnp.float32),
            pltpu.VMEM((rows, width // QUARTERS), jnp.float32),
            pltpu.VMEM((2, 1, width // QUARTERS), jnp.float32),
            pltpu.SemaphoreType.DMA((QUARTERS + 6,)),
            weight_buffer(up, QUARTERS),
            weight_sems(QUARTERS),
        ],
        {QUARTERS + 4 + i: 4 + i for i in range(4)},
        STAGE_BYTES,
        [(rows, width, local), (rows, local, width // 2)],
    )
    return (result[:2], result[2:4], result[4:8], result[8:])


def run_backward_far(section, place, pieces, kept, up, down, grads):
    rows, (local, width) = pieces[0].shape[0], up.shape
    part = struct(rows, width // QUARTERS + LANES)
    result = call(
        functools.partial(backward_far, section),
        [place, *pieces, *kept, up, down, *grads],
        [SMEM] + [VMEM] * (QUARTERS + 3) + [ANY] * 5,
        [
            part,
            part,
            struct(rows, local),
            struct(rows, LANES),
            struct(rows, width),
            struct(rows, local),
            struct(QUARTERS, 1, width // QUARTERS, dtype=jnp.float32),
        ],
        [VMEM] * 4 + [ANY] * 3,
        [
            pltpu.VMEM((2, 1, width // QUARTERS), jnp.float32),
            pltpu.SemaphoreType.DMA((QUARTERS + 3,)),
            weight_buffer(up, 2),
            weight_buffer(up, QUARTERS),
            weight_sems(2),
            weight_sems(QUARTERS),
        ],
        {QUARTERS + 6 + i: 4 + i for i in range(3)},
        STAGE_BYTES,
        [(rows, width, local), (rows, local, width // 2)],
    )
    return (result[:2], result[2:4], result[4:])


def run_backward_near(section, place, passed, kept, up, gain_part):
    rows, (local, width) = kept[0].shape[0], up.shape
    part = struct(rows, width // QUARTERS + LANES)
    result = call(
        functools.partial(backward_near, section),
        [place, *passed, kept[0], kept[1], up, gain_part],
        [SMEM] + [VMEM] * 4 + [ANY] * 2,
        [part, part, struct(*gain_part.shape, dtype=jnp.float32)],
        [VMEM, VMEM, ANY],
        [
            pltpu.VMEM((2, 1, width // QUARTERS), jnp.float32),
            pltpu.SemaphoreType.DMA((2,)),
            weight_buffer(up, 2),
            weight_sems(2),
        ],
        {6: 2},
        STAGE_BYTES,
        [(rows, local, width // 2)],
    )
    return (result[:2], result[2])


def run_final(section, place, pieces, grads, kept, gain, up, down):
    rows, (local, width) = pieces[0].shape[0], up.shape
    buffers = [
        pltpu.VMEM((SLOTS, BLOCK, width), jnp.float32),
        pltpu.SemaphoreType.DMA((SLOTS,)),
    ]
    grad_down, preact_grad, gain_part, scaled = call(
        functools.partial(final_down, section),
        [place, *pieces, *grads, *kept, gain, up, down],
        [SMEM] + [VMEM] * (QUARTERS + 7) + [ANY] * 2,
        [
            struct(local, width, dtype=jnp.float32),
            struct(rows, local),
            struct(*grads[2].shape, dtype=jnp.float32),
            struct(rows, width),
        ],
        [ANY] + [VMEM] * 3,
        [
            pltpu.VMEM((rows, width), jnp.bfloat16),
            pltpu.VMEM((rows, local), jnp.bfloat16),
            pltpu.VMEM((rows, local), jnp.float32),
            *buffers,
            weight_buffer(up, QUARTERS),
            weight_buffer(up, QUARTERS),
            weight_sems(QUARTERS),
            weight_sems(QUARTERS),
        ],
        {},
        FINAL_BYTES,
        [(rows, width, local)] * 2 + [(local, rows, width)],
    )
    blocks = hidden_blocks(local)
    half = (len(blocks) + 1) // 2
    grad_up = ()
    for taken in (blocks[:half], blocks[half:]):
        grad_up = call(
            functools.partial(final_up, taken),
            [preact_grad, scaled, *grad_up],
            [VMEM, VMEM] + [ANY] * len(grad_up),
            [struct(local, width, dtype=jnp.float32)],
            [ANY],
            buffers,
            {2: 0} if grad_up else {},
            FINAL_BYTES,
            [(local // 2, rows, width)],
        )
    return (grad_up[0], grad_down, gain_part)


def within(sections, flip):
    count = lax.axis_size("dp")
    return [(s * count + r, s * count + (r ^ flip)) for s in sections for r in range(count)]


def between(moves, flip):
    count = lax.axis_size("dp")
    return [(s * count + r, t * count + (r ^ flip)) for s, t in moves for r in range(count)]


def send_quarter(part, sections, k):
    return lax.ppermute(part, AXES, within(sections, k * (lax.axis_size("dp") // QUARTERS)))


def sum_quarters(own, arrived, sections):
    inner = lax.axis_size("dp") // QUARTERS
    total = own.astype(jnp.float32)
    for value in arrived:
        total = total + value.astype(jnp.float32)
    flip = 1
    while flip < inner:
        rounded = total.astype(jnp.bfloat16)
        other = lax.ppermute(rounded, AXES, within(sections, flip))
        total = rounded.astype(jnp.float32) + other.astype(jnp.float32)
        flip *= 2
    return total


def hand_on(own, moves):
    inner = lax.axis_size("dp") // QUARTERS
    pieces = {
        k: lax.ppermute(own, AXES, between(moves, k * inner)) for k in range(QUARTERS - 1, -1, -1)
    }
    return [pieces[k] for k in range(QUARTERS)]


def gather_chunks(chunk, sections, lows):
    held = chunk[None]
    for i, low in enumerate(lows):
        other = lax.ppermute(held, AXES, within(sections, 1 << i))
        held = jnp.concatenate([jnp.where(low, held, other), jnp.where(low, other, held)], axis=0)
    return held


def sum_over_dp(value):
    flip = 1
    while flip < lax.axis_size("dp"):
        value = value + lax.ppermute(
            value, "dp", [(r, r ^ flip) for r in range(lax.axis_size("dp"))]
        )
        flip *= 2
    return value


def body(section_input, out_cotangent, up_weight, down_weight, norm_gain):
    section_count = lax.axis_size("section")
    section_pos = lax.axis_index("section")
    count = lax.axis_size("dp")
    position = lax.axis_index("dp")
    outer_pos = position // (count // QUARTERS)
    width = up_weight.shape[1]
    quarter_width = width // QUARTERS
    last = section_count - 1

    def alike(section):
        return [s for s in range(section_count) if s % 2 == section % 2]

    def moves(section, step):
        return [(s, s + step) for s in alike(section) if 0 <= s + step < section_count]

    place = jnp.stack([section_pos, outer_pos]).astype(jnp.int32)
    lows = [(position >> i) % 2 == 0 for i in range(count.bit_length() - 1)]
    chunk = jnp.where(section_pos == last, out_cotangent, section_input)
    chunk, place, lows = lax.optimization_barrier((chunk, place, lows))
    held = gather_chunks(chunk, [0, last], lows)
    up = pltpu.with_memory_space_constraint(up_weight[0].T, pltpu.HBM)
    down = pltpu.with_memory_space_constraint(down_weight[0].T, pltpu.HBM)
    entered, own_entered, own_gain = run_lay_rows(place, held, norm_gain)

    pieces, stash, own = [entered], (), own_entered
    for section in range(last):
        here = alike(section)
        far, hidden, stash = run_forward_far(section, place, pieces, norm_gain, up, down, stash)
        arrived = [send_quarter(part, here, k) for part, k in zip(far, FAR)]
        near = run_forward_near(section, place, hidden, down)
        arrived.append(send_quarter(near[0], here, 1))
        result = own.astype(jnp.float32) + sum_quarters(near[1], arrived, here)
        pieces = hand_on(result.astype(jnp.bfloat16), moves(section, 1))
        own = pieces[0]
        if section == 0:
            grad_rows, early = run_early_grad(last, place, entered, down)

    for section in range(last, 0, -1):
        here = alike(section)
        if section == last:
            far, passed, stash, grads = run_last_far(
                last, place, pieces, early, norm_gain, up, stash
            )
            *stash, own_normed = stash
            own_scale = stash[1][:, :1]
            grads = [grad_rows, *grads]
            own = own_entered
        else:
            far, passed, grads = run_backward_far(section, place, pieces, stash, up, down, grads)
            own = pieces[0]
        arrived = [send_quarter(part, here, k) for part, k in zip(far, FAR)]
        near, gain_part = run_backward_near(section, place, passed, stash, up, grads[2])
        grads = [grads[0], grads[1], gain_part]
        arrived.append(send_quarter(near[0], here, 1))
        total = sum_quarters(near[1], arrived, here)
        along = total[:, quarter_width : quarter_width + 1] * (1.0 / width)
        normed_grad = total[:, :quarter_width] * own_gain
        result = own.astype(jnp.float32) + own_scale * (normed_grad - own_normed * along)
        pieces = hand_on(result.astype(jnp.bfloat16), moves(section, -1))

    grad_up, grad_down, gain_part = run_final(
        0, place, pieces, grads, stash, norm_gain, up, down
    )
    grad_gain = sum_over_dp(gain_part.reshape(1, width))
    return (grad_up.T[None], grad_down.T[None], grad_gain)


def solution(mesh):
    placed = (
        P(None, "dp", None),
        P(None, "dp", None),
        P("section", None, "dp"),
        P("section", None, "dp"),
        P("section", None),
    )
    return jax.shard_map(
        body,
        mesh=mesh,
        in_specs=placed,
        out_specs=(P("section", None, "dp"), P("section", None, "dp"), P("section", None)),
        check_vma=False,
    )
```

time: 812 us -> 367 us (0.45)
  starting transfers between devices: 422 us -> 114 us
  matrix products: 160 us -> 0 us
  waiting for transfers between devices: 41.5 us -> 178 us
  local copies, waits for them, and re-layouts: 94.4 us -> 0.86 us
  Pallas kernels: 0 us -> 59 us
  blocking collectives: 55.5 us -> 0 us
  other arithmetic: 24.7 us -> 6.08 us
    ppermute x86 -> x54, starting transfers between devices: 416 us -> 114 us  [the longest x24 46.3 us: hand_on(): lax.ppermute(own, AXES, between(moves, k * inner))]
    dot_general x17 -> x0, matrix products: 160 us -> none  [the longest x7 55.6 us: across_hidden(): lax.dot_general(left, right, (((1,), (1,)), ((), ())), preferred_element_...]
    ppermute x86 -> x54, waiting for transfers between devices: 21.8 us -> 178 us  [the longest x24 133 us: hand_on(): lax.ppermute(own, AXES, between(moves, k * inner))]
    concatenate x8 -> x0, local copies, waits for them, and re-layouts: 72.6 us -> none  [spread(): jnp.concatenate([send(chunk, source, target, k) for k in range(lax.axis_s...]
    pallas_call x0 -> x17, Pallas kernels: none -> 59 us  [call(): pl.pallas_call(kernel, out_shape=outputs, in_specs=specs, out_specs=out_s...]
    all_to_all x2 -> x0, blocking collectives: 55.5 us -> none  [collect_all(): arrived = lax.all_to_all(placed, 'dp', 0, 0, tiled=True)]
    all_to_all x1 -> x0, waiting for transfers between devices: 19.7 us -> none  [collect_all(): arrived = lax.all_to_all(placed, 'dp', 0, 0, tiled=True)]
    slice x12 -> x1, local copies, waits for them, and re-layouts: 12.4 us -> 0.11 us  [body(): own_scale = stash[1][:, :1]]
  transfers between devices with their start and end apart: 87 -> 54, of which waited for: 13 -> 18; matrix products, arithmetic and copies ran while one was open for 4% -> 0% of each run, Pallas kernels for 0% -> 6%
where the time goes in v3:
time: 367 us; the launch traced here: 360 us
  waiting for transfers between devices  178 us (49%)
  starting transfers between devices  114 us (31%)
  Pallas kernels  59 us (16%)
  other arithmetic  6.08 us (2%)
    ppermute x24, waiting for transfers between devices, hand_on(): lax.ppermute(own, AXES, between(moves, k * inner))  133 us
    pallas_call x17, Pallas kernels, call(): pl.pallas_call(kernel, out_shape=outputs, in_specs=specs, out_specs=out_s...  59 us
    ppermute x24, starting transfers between devices, hand_on(): lax.ppermute(own, AXES, between(moves, k * inner))  46.3 us
    ppermute x18, starting transfers between devices, send_quarter(): lax.ppermute(part, AXES, within(sections, k * (lax.axis_size('dp') // QUA...  36.6 us
    ppermute x18, waiting for transfers between devices, send_quarter(): lax.ppermute(part, AXES, within(sections, k * (lax.axis_size('dp') // QUA...  17.4 us
    ppermute x3, waiting for transfers between devices, gather_chunks(): other = lax.ppermute(held, AXES, within(sections, 1 << i))  14 us
    ppermute x3, starting transfers between devices, gather_chunks(): other = lax.ppermute(held, AXES, within(sections, 1 << i))  13.8 us
    ppermute x6, starting transfers between devices, sum_quarters(): other = lax.ppermute(rounded, AXES, within(sections, flip))  12.3 us
  transfers between devices with their start and end apart: 54, of which 18 were waited for; matrix products, arithmetic and copies ran while one was open for 0% of the time, Pallas kernels for 6%

profile of v3, /device:TPU:0, one launch (start us, length us, event | category | flops | bytes accessed | tf_op | source)
XLA Modules:
  0.0 359.5 jit_solution(5188627765518269238)
XLA Ops:
  1.7 4.9 %collective-permute-start = (bf16[1,3,2,6656]{3,2,1,0:T(2,128)(2,1)S(1)}, bf16[1,3,2,6656]{3,2,1,0:T(2,128)(2,1)S(1)}, u32[]{:S(2)}, u32[]{:S(2)}) collective-permute-start(bf16[1,3,2,6656]{3,2,1,0:T(2,128)(2,1)S(1)} %bitcast.41), channel_id=1, source_target_pairs={{0,1},{1,0},{2,3},{3,2},{4,5},{5,4},{6,7},{7,6},{24,25},{25,24},{2... | collective-permute-start | bytes 239624 | tf_op jit(solution)/shard_map/ppermute | solution.py:729
  9.4 4.0 %collective-permute-start.1 = (bf16[2,3,2,6656]{3,2,1,0:T(2,128)(2,1)S(1)}, bf16[2,3,2,6656]{3,2,1,0:T(2,128)(2,1)S(1)}, u32[]{:S(2)}, u32[]{:S(2)}) collective-permute-start(bf16[2,3,2,6656]{3,2,1,0:T(2,128)(2,1)S(1)} %pad_maximum_fusion.2), channel_id=1, source_target_pairs={{0,2},{1,3},{2,0},{3,1},{4,6},{5,7},{6,4},{7,5},{24,26},{25,27},{2... | collective-permute-start | bytes 479240 | tf_op jit(solution)/shard_map/ppermute | solution.py:729
  13.3 3.2 collective-permute-done.1
  17.4 4.9 %collective-permute-start.2 = (bf16[4,3,2,6656]{3,2,1,0:T(2,128)(2,1)S(1)}, bf16[4,3,2,6656]{3,2,1,0:T(2,128)(2,1)S(1)}, u32[]{:S(2)}, u32[]{:S(2)}) collective-permute-start(bf16[4,3,2,6656]{3,2,1,0:T(2,128)(2,1)S(1)} %pad_maximum_fusion.1), channel_id=1, source_target_pairs={{0,4},{1,5},{2,6},{3,7},{4,0},{5,1},{6,2},{7,3},{24,28},{25,29},{2... | collective-permute-start | bytes 958472 | tf_op jit(solution)/shard_map/ppermute | solution.py:729
  22.3 8.4 %collective-permute-done.2 = bf16[4,3,2,6656]{3,2,1,0:T(2,128)(2,1)S(1)} collective-permute-done((bf16[4,3,2,6656]{3,2,1,0:T(2,128)(2,1)S(1)}, bf16[4,3,2,6656]{3,2,1,0:T(2,128)(2,1)S(1)}, u32[]{:S(2)}, u32[]{:S(2)}) %collective-permute-start.2) | collective-permute-done | bytes 319520 | tf_op jit(solution)/shard_map/ppermute | solution.py:729
  33.9 10.7 %shard_map.77 = (bf16[48,1664]{1,0:T(8,128)(2,1)S(1)}, bf16[48,1664]{1,0:T(8,128)(2,1)S(1)}, bf16[48,1120]{1,0:T(8,128)(2,1)S(1)}, bf16[48,6656]{1,0:T(8,128)(2,...) custom-call(s32[2]{0:T(128)S(1)} %pad_add_fusion.place_ref, ...), custom_call_target="tpu_custom_call" | custom-call | flops 1073479680 | bytes 22364160 | tf_op jit(solution)/shard_map/pallas_call | solution.py:426
  44.6 5.7 %collective-permute-start.3 = (bf16[48,1664]{1,0:T(8,128)(2,1)S(1)}, bf16[48,1664]{1,0:T(8,128)(2,1)S(1)}, u32[]{:S(2)}, u32[]{:S(2)}) collective-permute-start(bf16[48,1664]{1,0:T(8,128)(2,1)S(1)} %get-tuple-element.86), channel_id=1, source_target_pairs={{0,6},{1,7},{2,4},{3,5},{4,2},{5,3},{6,0},{7,1},{16,22},{17,23},{1... | collective-permute-start | bytes 479240 | tf_op jit(solution)/shard_map/ppermute | solution.py:701
  52.3 4.5 %shard_map.78 = (bf16[48,1664]{1,0:T(8,128)(2,1)S(1)}, bf16[48,1664]{1,0:T(8,128)(2,1)S(1)}) custom-call(s32[2]{0:T(128)S(1)} %pad_add_fusion.place_ref, bf16[48,1120]{1,0:T(8,128)(2,1)S(1)} %get-tuple-element.84.hidden_ref, bf16[1120,6656]{1,0:T(8,128)(2,1)} %bitcast.31), custom_call_target="tpu_custom_call" | custom-call | flops 357826560 | bytes 7454720 | tf_op jit(solution)/shard_map/pallas_call | solution.py:426
  56.8 2.5 collective-permute-start.5
  59.3 4.7 %collective-permute-done.5 = bf16[48,1664]{1,0:T(8,128)(2,1)S(1)} collective-permute-done((bf16[48,1664]{1,0:T(8,128)(2,1)S(1)}, bf16[48,1664]{1,0:T(8,128)(2,1)S(1)}, u32[]{:S(2)}, u32[]{:S(2)}) %collective-permute-start.5) | collective-permute-done | bytes 159776 | tf_op jit(solution)/shard_map/ppermute | solution.py:701
  64.1 3.4 collective-permute-start.6
  67.5 3.7 %collective-permute-done.6 = bf16[48,1664]{1,0:T(8,128)(2,1)S(1)} collective-permute-done((bf16[48,1664]{1,0:T(8,128)(2,1)S(1)}, bf16[48,1664]{1,0:T(8,128)(2,1)S(1)}, u32[]{:S(2)}, u32[]{:S(2)}) %collective-permute-start.6) | collective-permute-done | bytes 159776 | tf_op jit(solution)/shard_map/ppermute | solution.py:712
  87.0 4.3 %collective-permute-start.19 = (bf16[48,1664]{1,0:T(8,128)(2,1)S(1)}, bf16[48,1664]{1,0:T(8,128)(2,1)S(1)}, u32[]{:S(2)}, u32[]{:S(2)}) collective-permute-start(bf16[48,1664]{1,0:T(8,128)(2,1)S(1)} %get-tuple-element.104), channel_id=1, source_target_pairs={{0,6},{1,7},{2,4},{3,5},{4,2},{5,3},{6,0},{7,1},{16,22},{17,23},{1... | collective-permute-start | bytes 479240 | tf_op jit(solution)/shard_map/ppermute | solution.py:701
  91.3 3.6 collective-permute-start.20
  95.5 2.5 collective-permute-start.21
  98.0 8.7 %collective-permute-done.20 = bf16[48,1664]{1,0:T(8,128)(2,1)S(1)} collective-permute-done((bf16[48,1664]{1,0:T(8,128)(2,1)S(1)}, bf16[48,1664]{1,0:T(8,128)(2,1)S(1)}, u32[]{:S(2)}, u32[]{:S(2)}) %collective-permute-start.20) | collective-permute-done | bytes 159776 | tf_op jit(solution)/shard_map/ppermute | solution.py:701
  106.8 3.4 collective-permute-start.22
  110.2 3.7 %collective-permute-done.22 = bf16[48,1664]{1,0:T(8,128)(2,1)S(1)} collective-permute-done((bf16[48,1664]{1,0:T(8,128)(2,1)S(1)}, bf16[48,1664]{1,0:T(8,128)(2,1)S(1)}, u32[]{:S(2)}, u32[]{:S(2)}) %collective-permute-start.22) | collective-permute-done | bytes 159776 | tf_op jit(solution)/shard_map/ppermute | solution.py:712
  114.0 19.3 %collective-permute-start.26 = (bf16[48,1664]{1,0:T(8,128)(2,1)S(1)}, bf16[48,1664]{1,0:T(8,128)(2,1)S(1)}, u32[]{:S(2)}, u32[]{:S(2)}) collective-permute-start(bf16[48,1664]{1,0:T(8,128)(2,1)S(1)} %add_convert_fusion.3), channel_id=1, source_target_pairs={{0,14},{1,15},{2,12},{3,13},{4,10},{5,11},{6,8},{7,9},{16,30},{17,... | collective-permute-start | bytes 479240 | tf_op jit(solution)/shard_map/ppermute | solution.py:721
  133.3 3.5 collective-permute-start.25
  151.1 18.9 %collective-permute-done.34.refs_3_ = bf16[48,1664]{1,0:T(8,128)(2,1)S(1)} collective-permute-done((bf16[48,1664]{1,0:T(8,128)(2,1)S(1)}, bf16[48,1664]{1,0:T(8,128)(2,1)S(1)}, u32[]{:S(2)}, u32[]{:S(2)}) %collective-permute-start.34) | collective-permute-done | bytes 159776 | tf_op jit(solution)/shard_map/ppermute | solution.py:721
  170.1 4.4 %collective-permute-done.33.refs_2_ = bf16[48,1664]{1,0:T(8,128)(2,1)S(1)} collective-permute-done((bf16[48,1664]{1,0:T(8,128)(2,1)S(1)}, bf16[48,1664]{1,0:T(8,128)(2,1)S(1)}, u32[]{:S(2)}, u32[]{:S(2)}) %collective-permute-start.33) | collective-permute-done | bytes 159776 | tf_op jit(solution)/shard_map/ppermute | solution.py:721
  175.4 4.4 %collective-permute-start.35 = (bf16[48,1792]{1,0:T(8,128)(2,1)S(1)}, bf16[48,1792]{1,0:T(8,128)(2,1)S(1)}, u32[]{:S(2)}, u32[]{:S(2)}) collective-permute-start(bf16[48,1792]{1,0:T(8,128)(2,1)S(1)} %get-tuple-element.131), channel_id=1, source_target_pairs={{0,6},{1,7},{2,4},{3,5},{4,2},{5,3},{6,0},{7,1},{16,22},{17,23},{1... | collective-permute-start | bytes 516104 | tf_op jit(solution)/shard_map/ppermute | solution.py:701
  182.3 3.8 %collective-permute-start.37 = (bf16[48,1792]{1,0:T(8,128)(2,1)S(1)}, bf16[48,1792]{1,0:T(8,128)(2,1)S(1)}, u32[]{:S(2)}, u32[]{:S(2)}) collective-permute-start(bf16[48,1792]{1,0:T(8,128)(2,1)S(1)} %get-tuple-element.133), channel_id=1, source_target_pairs={{0,2},{1,3},{2,0},{3,1},{4,6},{5,7},{6,4},{7,5},{16,18},{17,19},{1... | collective-permute-start | bytes 516104 | tf_op jit(solution)/shard_map/ppermute | solution.py:701
  190.2 3.4 collective-permute-start.38
  193.6 3.9 %collective-permute-done.38 = bf16[48,1792]{1,0:T(8,128)(2,1)S(1)} collective-permute-done((bf16[48,1792]{1,0:T(8,128)(2,1)S(1)}, bf16[48,1792]{1,0:T(8,128)(2,1)S(1)}, u32[]{:S(2)}, u32[]{:S(2)}) %collective-permute-start.38) | collective-permute-done | bytes 172064 | tf_op jit(solution)/shard_map/ppermute | solution.py:712
  210.2 101.0 %collective-permute-done.50.refs_3_ = bf16[48,1664]{1,0:T(8,128)(2,1)S(1)} collective-permute-done((bf16[48,1664]{1,0:T(8,128)(2,1)S(1)}, bf16[48,1664]{1,0:T(8,128)(2,1)S(1)}, u32[]{:S(2)}, u32[]{:S(2)}) %collective-permute-start.50) | collective-permute-done | bytes 159776 | tf_op jit(solution)/shard_map/ppermute | solution.py:721
  311.2 5.0 %collective-permute-done.49.refs_2_ = bf16[48,1664]{1,0:T(8,128)(2,1)S(1)} collective-permute-done((bf16[48,1664]{1,0:T(8,128)(2,1)S(1)}, bf16[48,1664]{1,0:T(8,128)(2,1)S(1)}, u32[]{:S(2)}, u32[]{:S(2)}) %collective-permute-start.49) | collective-permute-done | bytes 159776 | tf_op jit(solution)/shard_map/ppermute | solution.py:721
  316.2 23.0 %shard_map.90 = (f32[1120,6656]{1,0:T(8,128)}, bf16[48,1120]{1,0:T(8,128)(2,1)S(1)}, f32[4,1,1664]{2,1,0:T(1,128)S(1)}, bf16[48,6656]{1,0:T(8,128)(2,1)S(1)}) custom-call(s32[2]{0:T(128)S(1)} %pad_add_fusion.place_ref, bf16[48,1664]{1,0:T(8,128)(2,1)S(1)} %collective-permute-done.47.refs_0_, bf16[48,1664]{1,0:T(8,128)(2,1)S(1)} %collective-permute-done.48.refs_1_, ...), custom_call_target="tpu_custom_call" | custom-call | flops 2146959360 | bytes 30457856 | tf_op jit(solution)/shard_map/pallas_call | solution.py:426
  343.3 6.7 %shard_map.91.refs_0_ = f32[1120,6656]{1,0:T(8,128)} custom-call(bf16[48,1120]{1,0:T(8,128)(2,1)S(1)} %get-tuple-element.147.preact_grad_ref, bf16[48,6656]{1,0:T(8,128)(2,1)S(1)} %get-tuple-element.148.scaled_ref), custom_call_target="tpu_custom_call" | custom-call | flops 357826560 | bytes 638976 | tf_op jit(solution)/shard_map/pallas_call | solution.py:426
  350.0 3.0 collective-permute-start.53
  353.0 5.4 %shard_map.92 = f32[1120,6656]{1,0:T(8,128)} custom-call(bf16[48,1120]{1,0:T(8,128)(2,1)S(1)} %get-tuple-element.147.preact_grad_ref, bf16[48,6656]{1,0:T(8,128)(2,1)S(1)} %get-tuple-element.148.scaled_ref, f32[1120,6656]{1,0:T(8,128)} %shard_map.91.refs_0_), custom_call_target="tpu_custom_call", output_to_operand_aliasing={{}: (2, {})} | custom-call | flops 357826560 | bytes 638976 | tf_op jit(solution)/shard_map/pallas_call | solution.py:426
  (132 shorter events, 64.8 us)
Async XLA Ops:
  1.7 7.3 %collective-permute-start = (bf16[1,3,2,6656]{3,2,1,0:T(2,128)(2,1)S(1)}, bf16[1,3,2,6656]{3,2,1,0:T(2,128)(2,1)S(1)}, u32[]{:S(2)}, u32[]{:S(2)}) collective-permute-start(bf16[1,3,2,6656]{3,2,1,0:T(2,128)(2,1)S(1)} %bitcast.41), channel_id=1, source_target_pairs={{0,1},{1,0},{2,3},{3,2},{4,5},{5,4},{6,7},{7,6},{24,25},{25,24},{2... | collective-permute-start | bytes 239624 | tf_op jit(solution)/shard_map/ppermute | solution.py:729
  9.4 7.2 %collective-permute-start.1 = (bf16[2,3,2,6656]{3,2,1,0:T(2,128)(2,1)S(1)}, bf16[2,3,2,6656]{3,2,1,0:T(2,128)(2,1)S(1)}, u32[]{:S(2)}, u32[]{:S(2)}) collective-permute-start(bf16[2,3,2,6656]{3,2,1,0:T(2,128)(2,1)S(1)} %pad_maximum_fusion.2), channel_id=1, source_target_pairs={{0,2},{1,3},{2,0},{3,1},{4,6},{5,7},{6,4},{7,5},{24,26},{25,27},{2... | collective-permute-start | bytes 479240 | tf_op jit(solution)/shard_map/ppermute | solution.py:729
  17.4 13.3 %collective-permute-start.2 = (bf16[4,3,2,6656]{3,2,1,0:T(2,128)(2,1)S(1)}, bf16[4,3,2,6656]{3,2,1,0:T(2,128)(2,1)S(1)}, u32[]{:S(2)}, u32[]{:S(2)}) collective-permute-start(bf16[4,3,2,6656]{3,2,1,0:T(2,128)(2,1)S(1)} %pad_maximum_fusion.1), channel_id=1, source_target_pairs={{0,4},{1,5},{2,6},{3,7},{4,0},{5,1},{6,2},{7,3},{24,28},{25,29},{2... | collective-permute-start | bytes 958472 | tf_op jit(solution)/shard_map/ppermute | solution.py:729
  44.6 14.7 %collective-permute-start.3 = (bf16[48,1664]{1,0:T(8,128)(2,1)S(1)}, bf16[48,1664]{1,0:T(8,128)(2,1)S(1)}, u32[]{:S(2)}, u32[]{:S(2)}) collective-permute-start(bf16[48,1664]{1,0:T(8,128)(2,1)S(1)} %get-tuple-element.86), channel_id=1, source_target_pairs={{0,6},{1,7},{2,4},{3,5},{4,2},{5,3},{6,0},{7,1},{16,22},{17,23},{1... | collective-permute-start | bytes 479240 | tf_op jit(solution)/shard_map/ppermute | solution.py:701
  50.4 9.0 %collective-permute-start.4 = (bf16[48,1664]{1,0:T(8,128)(2,1)S(1)}, bf16[48,1664]{1,0:T(8,128)(2,1)S(1)}, u32[]{:S(2)}, u32[]{:S(2)}) collective-permute-start(bf16[48,1664]{1,0:T(8,128)(2,1)S(1)} %get-tuple-element.87), channel_id=1, source_target_pairs={{0,4},{1,5},{2,6},{3,7},{4,0},{5,1},{6,2},{7,3},{16,20},{17,21},{1... | collective-permute-start | bytes 479240 | tf_op jit(solution)/shard_map/ppermute | solution.py:701
  56.8 7.2 %collective-permute-start.5 = (bf16[48,1664]{1,0:T(8,128)(2,1)S(1)}, bf16[48,1664]{1,0:T(8,128)(2,1)S(1)}, u32[]{:S(2)}, u32[]{:S(2)}) collective-permute-start(bf16[48,1664]{1,0:T(8,128)(2,1)S(1)} %get-tuple-element.88), channel_id=1, source_target_pairs={{0,2},{1,3},{2,0},{3,1},{4,6},{5,7},{6,4},{7,5},{16,18},{17,19},{1... | collective-permute-start | bytes 479240 | tf_op jit(solution)/shard_map/ppermute | solution.py:701
  64.1 7.2 %collective-permute-start.6 = (bf16[48,1664]{1,0:T(8,128)(2,1)S(1)}, bf16[48,1664]{1,0:T(8,128)(2,1)S(1)}, u32[]{:S(2)}, u32[]{:S(2)}) collective-permute-start(bf16[48,1664]{1,0:T(8,128)(2,1)S(1)} %add_convert_fusion.7), channel_id=1, source_target_pairs={{0,1},{1,0},{2,3},{3,2},{4,5},{5,4},{6,7},{7,6},{16,17},{17,16},{1... | collective-permute-start | bytes 479240 | tf_op jit(solution)/shard_map/ppermute | solution.py:712
  71.3 5.2 %collective-permute-start.10 = (bf16[48,1664]{1,0:T(8,128)(2,1)S(1)}, bf16[48,1664]{1,0:T(8,128)(2,1)S(1)}, u32[]{:S(2)}, u32[]{:S(2)}) collective-permute-start(bf16[48,1664]{1,0:T(8,128)(2,1)S(1)} %fusion), channel_id=1, source_target_pairs={{0,14},{1,15},{2,12},{3,13},{4,10},{5,11},{6,8},{7,9},{16,30},{17,... | collective-permute-start | bytes 479240 | tf_op jit(solution)/shard_map/ppermute | solution.py:721
  72.7 4.5 %collective-permute-start.9 = (bf16[48,1664]{1,0:T(8,128)(2,1)S(1)}, bf16[48,1664]{1,0:T(8,128)(2,1)S(1)}, u32[]{:S(2)}, u32[]{:S(2)}) collective-permute-start(bf16[48,1664]{1,0:T(8,128)(2,1)S(1)} %fusion), channel_id=1, source_target_pairs={{0,12},{1,13},{2,14},{3,15},{4,8},{5,9},{6,10},{7,11},{16,28},{17,... | collective-permute-start | bytes 479240 | tf_op jit(solution)/shard_map/ppermute | solution.py:721
  74.0 4.9 %collective-permute-start.8 = (bf16[48,1664]{1,0:T(8,128)(2,1)S(1)}, bf16[48,1664]{1,0:T(8,128)(2,1)S(1)}, u32[]{:S(2)}, u32[]{:S(2)}) collective-permute-start(bf16[48,1664]{1,0:T(8,128)(2,1)S(1)} %fusion), channel_id=1, source_target_pairs={{0,10},{1,11},{2,8},{3,9},{4,14},{5,15},{6,12},{7,13},{16,26},{17,... | collective-permute-start | bytes 479240 | tf_op jit(solution)/shard_map/ppermute | solution.py:721
  87.0 10.9 %collective-permute-start.19 = (bf16[48,1664]{1,0:T(8,128)(2,1)S(1)}, bf16[48,1664]{1,0:T(8,128)(2,1)S(1)}, u32[]{:S(2)}, u32[]{:S(2)}) collective-permute-start(bf16[48,1664]{1,0:T(8,128)(2,1)S(1)} %get-tuple-element.104), channel_id=1, source_target_pairs={{0,6},{1,7},{2,4},{3,5},{4,2},{5,3},{6,0},{7,1},{16,22},{17,23},{1... | collective-permute-start | bytes 479240 | tf_op jit(solution)/shard_map/ppermute | solution.py:701
  91.3 15.4 %collective-permute-start.20 = (bf16[48,1664]{1,0:T(8,128)(2,1)S(1)}, bf16[48,1664]{1,0:T(8,128)(2,1)S(1)}, u32[]{:S(2)}, u32[]{:S(2)}) collective-permute-start(bf16[48,1664]{1,0:T(8,128)(2,1)S(1)} %get-tuple-element.105), channel_id=1, source_target_pairs={{0,4},{1,5},{2,6},{3,7},{4,0},{5,1},{6,2},{7,3},{16,20},{17,21},{1... | collective-permute-start | bytes 479240 | tf_op jit(solution)/shard_map/ppermute | solution.py:701
  95.5 11.2 %collective-permute-start.21 = (bf16[48,1664]{1,0:T(8,128)(2,1)S(1)}, bf16[48,1664]{1,0:T(8,128)(2,1)S(1)}, u32[]{:S(2)}, u32[]{:S(2)}) collective-permute-start(bf16[48,1664]{1,0:T(8,128)(2,1)S(1)} %get-tuple-element.106), channel_id=1, source_target_pairs={{0,2},{1,3},{2,0},{3,1},{4,6},{5,7},{6,4},{7,5},{16,18},{17,19},{1... | collective-permute-start | bytes 479240 | tf_op jit(solution)/shard_map/ppermute | solution.py:701
  106.8 7.2 %collective-permute-start.22 = (bf16[48,1664]{1,0:T(8,128)(2,1)S(1)}, bf16[48,1664]{1,0:T(8,128)(2,1)S(1)}, u32[]{:S(2)}, u32[]{:S(2)}) collective-permute-start(bf16[48,1664]{1,0:T(8,128)(2,1)S(1)} %add_convert_fusion.4), channel_id=1, source_target_pairs={{0,1},{1,0},{2,3},{3,2},{4,5},{5,4},{6,7},{7,6},{16,17},{17,16},{1... | collective-permute-start | bytes 479240 | tf_op jit(solution)/shard_map/ppermute | solution.py:712
  114.0 26.2 %collective-permute-start.26 = (bf16[48,1664]{1,0:T(8,128)(2,1)S(1)}, bf16[48,1664]{1,0:T(8,128)(2,1)S(1)}, u32[]{:S(2)}, u32[]{:S(2)}) collective-permute-start(bf16[48,1664]{1,0:T(8,128)(2,1)S(1)} %add_convert_fusion.3), channel_id=1, source_target_pairs={{0,14},{1,15},{2,12},{3,13},{4,10},{5,11},{6,8},{7,9},{16,30},{17,... | collective-permute-start | bytes 479240 | tf_op jit(solution)/shard_map/ppermute | solution.py:721
  133.3 6.9 %collective-permute-start.25 = (bf16[48,1664]{1,0:T(8,128)(2,1)S(1)}, bf16[48,1664]{1,0:T(8,128)(2,1)S(1)}, u32[]{:S(2)}, u32[]{:S(2)}) collective-permute-start(bf16[48,1664]{1,0:T(8,128)(2,1)S(1)} %add_convert_fusion.3), channel_id=1, source_target_pairs={{0,12},{1,13},{2,14},{3,15},{4,8},{5,9},{6,10},{7,11},{16,28},{17,... | collective-permute-start | bytes 479240 | tf_op jit(solution)/shard_map/ppermute | solution.py:721
  136.8 4.5 %collective-permute-start.24 = (bf16[48,1664]{1,0:T(8,128)(2,1)S(1)}, bf16[48,1664]{1,0:T(8,128)(2,1)S(1)}, u32[]{:S(2)}, u32[]{:S(2)}) collective-permute-start(bf16[48,1664]{1,0:T(8,128)(2,1)S(1)} %add_convert_fusion.3), channel_id=1, source_target_pairs={{0,10},{1,11},{2,8},{3,9},{4,14},{5,15},{6,12},{7,13},{16,26},{17,... | collective-permute-start | bytes 479240 | tf_op jit(solution)/shard_map/ppermute | solution.py:721
  145.9 24.1 %collective-permute-start.34 = (bf16[48,1664]{1,0:T(8,128)(2,1)S(1)}, bf16[48,1664]{1,0:T(8,128)(2,1)S(1)}, u32[]{:S(2)}, u32[]{:S(2)}) collective-permute-start(bf16[48,1664]{1,0:T(8,128)(2,1)S(1)} %fusion.1), channel_id=1, source_target_pairs={{8,6},{9,7},{10,4},{11,5},{12,2},{13,3},{14,0},{15,1},{24,22},{25,... | collective-permute-start | bytes 479240 | tf_op jit(solution)/shard_map/ppermute | solution.py:721
  147.2 27.3 %collective-permute-start.33 = (bf16[48,1664]{1,0:T(8,128)(2,1)S(1)}, bf16[48,1664]{1,0:T(8,128)(2,1)S(1)}, u32[]{:S(2)}, u32[]{:S(2)}) collective-permute-start(bf16[48,1664]{1,0:T(8,128)(2,1)S(1)} %fusion.1), channel_id=1, source_target_pairs={{8,4},{9,5},{10,6},{11,7},{12,0},{13,1},{14,2},{15,3},{24,20},{25,... | collective-permute-start | bytes 479240 | tf_op jit(solution)/shard_map/ppermute | solution.py:721
  148.5 26.0 %collective-permute-start.32 = (bf16[48,1664]{1,0:T(8,128)(2,1)S(1)}, bf16[48,1664]{1,0:T(8,128)(2,1)S(1)}, u32[]{:S(2)}, u32[]{:S(2)}) collective-permute-start(bf16[48,1664]{1,0:T(8,128)(2,1)S(1)} %fusion.1), channel_id=1, source_target_pairs={{8,2},{9,3},{10,0},{11,1},{12,6},{13,7},{14,4},{15,5},{24,18},{25,... | collective-permute-start | bytes 479240 | tf_op jit(solution)/shard_map/ppermute | solution.py:721
  149.8 24.7 %collective-permute-start.31 = (bf16[48,1664]{1,0:T(8,128)(2,1)S(1)}, bf16[48,1664]{1,0:T(8,128)(2,1)S(1)}, u32[]{:S(2)}, u32[]{:S(2)}) collective-permute-start(bf16[48,1664]{1,0:T(8,128)(2,1)S(1)} %fusion.1), channel_id=1, source_target_pairs={{8,0},{9,1},{10,2},{11,3},{12,4},{13,5},{14,6},{15,7},{24,16},{25,... | collective-permute-start | bytes 479240 | tf_op jit(solution)/shard_map/ppermute | solution.py:721
  175.4 10.7 %collective-permute-start.35 = (bf16[48,1792]{1,0:T(8,128)(2,1)S(1)}, bf16[48,1792]{1,0:T(8,128)(2,1)S(1)}, u32[]{:S(2)}, u32[]{:S(2)}) collective-permute-start(bf16[48,1792]{1,0:T(8,128)(2,1)S(1)} %get-tuple-element.131), channel_id=1, source_target_pairs={{0,6},{1,7},{2,4},{3,5},{4,2},{5,3},{6,0},{7,1},{16,22},{17,23},{1... | collective-permute-start | bytes 516104 | tf_op jit(solution)/shard_map/ppermute | solution.py:701
  179.8 8.6 %collective-permute-start.36 = (bf16[48,1792]{1,0:T(8,128)(2,1)S(1)}, bf16[48,1792]{1,0:T(8,128)(2,1)S(1)}, u32[]{:S(2)}, u32[]{:S(2)}) collective-permute-start(bf16[48,1792]{1,0:T(8,128)(2,1)S(1)} %get-tuple-element.132), channel_id=1, source_target_pairs={{0,4},{1,5},{2,6},{3,7},{4,0},{5,1},{6,2},{7,3},{16,20},{17,21},{1... | collective-permute-start | bytes 516104 | tf_op jit(solution)/shard_map/ppermute | solution.py:701
  182.3 7.8 %collective-permute-start.37 = (bf16[48,1792]{1,0:T(8,128)(2,1)S(1)}, bf16[48,1792]{1,0:T(8,128)(2,1)S(1)}, u32[]{:S(2)}, u32[]{:S(2)}) collective-permute-start(bf16[48,1792]{1,0:T(8,128)(2,1)S(1)} %get-tuple-element.133), channel_id=1, source_target_pairs={{0,2},{1,3},{2,0},{3,1},{4,6},{5,7},{6,4},{7,5},{16,18},{17,19},{1... | collective-permute-start | bytes 516104 | tf_op jit(solution)/shard_map/ppermute | solution.py:701
  190.2 7.3 %collective-permute-start.38 = (bf16[48,1792]{1,0:T(8,128)(2,1)S(1)}, bf16[48,1792]{1,0:T(8,128)(2,1)S(1)}, u32[]{:S(2)}, u32[]{:S(2)}) collective-permute-start(bf16[48,1792]{1,0:T(8,128)(2,1)S(1)} %add_convert_fusion.1), channel_id=1, source_target_pairs={{0,1},{1,0},{2,3},{3,2},{4,5},{5,4},{6,7},{7,6},{16,17},{17,16},{1... | collective-permute-start | bytes 516104 | tf_op jit(solution)/shard_map/ppermute | solution.py:712
  205.0 106.2 %collective-permute-start.50 = (bf16[48,1664]{1,0:T(8,128)(2,1)S(1)}, bf16[48,1664]{1,0:T(8,128)(2,1)S(1)}, u32[]{:S(2)}, u32[]{:S(2)}) collective-permute-start(bf16[48,1664]{1,0:T(8,128)(2,1)S(1)} %fusion.5), channel_id=1, source_target_pairs={{8,6},{9,7},{10,4},{11,5},{12,2},{13,3},{14,0},{15,1},{24,22},{25,... | collective-permute-start | bytes 479240 | tf_op jit(solution)/shard_map/ppermute | solution.py:721
  206.3 109.9 %collective-permute-start.49 = (bf16[48,1664]{1,0:T(8,128)(2,1)S(1)}, bf16[48,1664]{1,0:T(8,128)(2,1)S(1)}, u32[]{:S(2)}, u32[]{:S(2)}) collective-permute-start(bf16[48,1664]{1,0:T(8,128)(2,1)S(1)} %fusion.5), channel_id=1, source_target_pairs={{8,4},{9,5},{10,6},{11,7},{12,0},{13,1},{14,2},{15,3},{24,20},{25,... | collective-permute-start | bytes 479240 | tf_op jit(solution)/shard_map/ppermute | solution.py:721
  207.6 108.6 %collective-permute-start.48 = (bf16[48,1664]{1,0:T(8,128)(2,1)S(1)}, bf16[48,1664]{1,0:T(8,128)(2,1)S(1)}, u32[]{:S(2)}, u32[]{:S(2)}) collective-permute-start(bf16[48,1664]{1,0:T(8,128)(2,1)S(1)} %fusion.5), channel_id=1, source_target_pairs={{8,2},{9,3},{10,0},{11,1},{12,6},{13,7},{14,4},{15,5},{24,18},{25,... | collective-permute-start | bytes 479240 | tf_op jit(solution)/shard_map/ppermute | solution.py:721
  208.9 107.3 %collective-permute-start.47 = (bf16[48,1664]{1,0:T(8,128)(2,1)S(1)}, bf16[48,1664]{1,0:T(8,128)(2,1)S(1)}, u32[]{:S(2)}, u32[]{:S(2)}) collective-permute-start(bf16[48,1664]{1,0:T(8,128)(2,1)S(1)} %fusion.5), channel_id=1, source_target_pairs={{8,0},{9,1},{10,2},{11,3},{12,4},{13,5},{14,6},{15,7},{24,16},{25,... | collective-permute-start | bytes 479240 | tf_op jit(solution)/shard_map/ppermute | solution.py:721
  339.2 3.9 %collective-permute-start.51 = (f32[1,6656]{1,0:T(1,128)S(1)}, f32[1,6656]{1,0:T(1,128)S(1)}, u32[]{:S(2)}, u32[]{:S(2)}) collective-permute-start(f32[1,6656]{1,0:T(1,128)S(1)} %bitcast.18), channel_id=1, source_target_pairs={{0,1},{1,0},{2,3},{3,2},{4,5},{5,4},{6,7},{7,6},{8,9},{9,8},{10,11... | collective-permute-start | bytes 79880 | tf_op jit(solution)/shard_map/ppermute | solution.py:737
  343.2 6.8 %collective-permute-start.52 = (f32[1,6656]{1,0:T(1,128)S(1)}, f32[1,6656]{1,0:T(1,128)S(1)}, u32[]{:S(2)}, u32[]{:S(2)}) collective-permute-start(f32[1,6656]{1,0:T(1,128)S(1)} %add.143), channel_id=1, source_target_pairs={{0,2},{1,3},{2,0},{3,1},{4,6},{5,7},{6,4},{7,5},{8,10},{9,11},{10,... | collective-permute-start | bytes 79880 | tf_op jit(solution)/shard_map/ppermute | solution.py:737
  350.0 8.4 %collective-permute-start.53 = (f32[1,6656]{1,0:T(1,128)S(1)}, f32[1,6656]{1,0:T(1,128)S(1)}, u32[]{:S(2)}, u32[]{:S(2)}) collective-permute-start(f32[1,6656]{1,0:T(1,128)S(1)} %add.144), channel_id=1, source_target_pairs={{0,4},{1,5},{2,6},{3,7},{4,0},{5,1},{6,2},{7,3},{8,12},{9,13},{10,... | collective-permute-start | bytes 79880 | tf_op jit(solution)/shard_map/ppermute | solution.py:737
  (26 other events, 348.9 us)
